TPU v7x, 256 devices: a whole 4x4x8 slice. The times are simulated.
256 devices in a mesh: ctx: 64 (over y, z, core), tp: 4 (over x).
Axes of the slice: x: 4, y: 4, z: 8, core: 2. Of those that a mesh axis runs over, the one named last changes fastest.
Arguments:
- frames: bfloat16 [16384, 2, 1024], P(('ctx', 'tp')), may hold values from -6 to 6
- lengths: int32 [2], replicated, may hold values from 8192 to 16384
- value_weight: bfloat16 [2, 1024, 1024], P(None, None, 'tp'), may hold values from -0.1875 to 0.1875
- gate_weight: bfloat16 [2, 1024, 1024], P(None, None, 'tp'), may hold values from -0.1875 to 0.1875
- tap_weights: float32 [2, 31, 1024], P(None, None, 'tp'), may hold values from -1 to 1
- norm_gain: float32 [2, 1024], P(None, 'tp'), may hold values from 0.5 to 2
- norm_shift: float32 [2, 1024], P(None, 'tp'), may hold values from -3 to 3
- project_weight: bfloat16 [2, 1024, 1024], P(None, 'tp'), may hold values from -0.1875 to 0.1875
- output_grad: bfloat16 [16384, 2, 1024], P(('ctx', 'tp')), may hold values from -6 to 6
Outputs:
- input_grad: float32 [16384, 2, 1024], P(('ctx', 'tp'))
- value_grad: float32 [2, 1024, 1024], P(None, 'ctx', 'tp')
- gate_grad: float32 [2, 1024, 1024], P(None, 'ctx', 'tp')
- project_grad: float32 [2, 1024, 1024], P(None, 'tp', 'ctx')
- tap_grad: float32 [2, 31, 1024], P(None, None, 'tp')
All inputs are finite; a program needn't handle non-finite values.
Results may differ from a plain program's by a relative error of at most 0.025.
Values may be sent and summed in bfloat16 or wider, within the bound.
A program may use at most 128 MiB of HBM per device.

v0:
```python
import jax
import jax.numpy as jnp
from jax import lax
from jax.sharding import PartitionSpec as P

EPSILON = 1e-05


def padded(block, sides, width):
    for axis, dim in sides:
        count = lax.axis_size(axis)
        forward = [(i, i + 1) for i in range(count - 1)]
        backward = [(target, source) for source, target in forward]
        low = lax.ppermute(
            lax.slice_in_dim(block, block.shape[dim] - width, None, axis=dim), axis, forward
        )
        high = lax.ppermute(lax.slice_in_dim(block, 0, width, axis=dim), axis, backward)
        block = jnp.concatenate([low, block, high], axis=dim)
    return block


def on_device(
    frames,
    lengths,
    value_weight,
    gate_weight,
    tap_weights,
    norm_gain,
    norm_shift,
    project_weight,
    output_grad,
):
    local_rows = frames.shape[0]
    frame_count = local_rows * lax.axis_size("tp")
    reach = tap_weights.shape[1] // 2
    layer_count = value_weight.shape[0]
    first_frame = lax.axis_index("ctx") * frame_count
    positions = first_frame + jnp.arange(frame_count, dtype=jnp.int32)[:, None]
    valid = (positions < lengths[None, :]).astype(jnp.float32)[:, :, None]
    total = jnp.sum(lengths).astype(jnp.float32)
    stored_list = []
    hidden = frames
    for layer in range(layer_count):
        rows32 = hidden.astype(jnp.float32)
        centered = rows32 - jnp.mean(rows32, axis=-1, keepdims=True)
        forward_ln_scale = lax.rsqrt(
            jnp.mean(centered * centered, axis=-1, keepdims=True) + EPSILON
        )
        forward_normed = centered * forward_ln_scale
        normed_low = forward_normed.astype(jnp.bfloat16)
        forward_gathered = lax.all_gather(normed_low, "tp", axis=0, tiled=True)
        forward_value_pre = jnp.einsum(
            "tbd,dc->tbc", forward_gathered, value_weight[layer], preferred_element_type=jnp.float32
        )
        forward_gate_pre = jnp.einsum(
            "tbd,dc->tbc", forward_gathered, gate_weight[layer], preferred_element_type=jnp.float32
        )
        glu = (forward_value_pre * jax.nn.sigmoid(forward_gate_pre) * valid).astype(jnp.bfloat16)
        forward_widened = padded(glu, (("ctx", 0),), reach).astype(jnp.float32)
        forward_taps = tap_weights[layer]
        mixed = forward_taps[0] * forward_widened[0:frame_count]
        for forward_offset in range(1, 2 * reach + 1):
            mixed = (
                mixed
                + forward_taps[forward_offset]
                * forward_widened[forward_offset : forward_offset + frame_count]
            )
        chan_mean = lax.psum(jnp.sum(mixed * valid, axis=(0, 1)), "ctx") / total
        chan_var = lax.psum(jnp.sum(((mixed - chan_mean) * valid) ** 2, axis=(0, 1)), "ctx") / total
        forward_chan_scale = lax.rsqrt(chan_var + EPSILON)
        forward_scaled = (mixed - chan_mean) * forward_chan_scale
        forward_shifted = norm_gain[layer] * forward_scaled + norm_shift[layer]
        forward_activated = (jax.nn.silu(forward_shifted) * valid).astype(jnp.bfloat16)
        rows32, stored = (
            rows32,
            (
                forward_normed,
                forward_ln_scale,
                forward_gathered,
                forward_value_pre,
                forward_gate_pre,
                forward_widened,
                forward_scaled,
                forward_shifted,
                forward_chan_scale,
                forward_activated,
            ),
        )
        stored_list.append(stored)
        if layer + 1 < layer_count:
            activated = stored[9]
            branch = lax.psum_scatter(
                jnp.einsum(
                    "tbc,cd->tbd",
                    activated,
                    project_weight[layer],
                    preferred_element_type=jnp.float32,
                ).astype(jnp.bfloat16),
                "tp",
                scatter_dimension=0,
                tiled=True,
            ).astype(jnp.float32)
            hidden = (rows32 + branch).astype(jnp.bfloat16)
    upstream = output_grad.astype(jnp.float32)
    value_list, gate_list, project_list, tap_list = ([], [], [], [])
    for layer in range(layer_count - 1, -1, -1):
        backward_stored = stored_list[layer]
        (
            normed,
            ln_scale,
            gathered,
            value_pre,
            gate_pre,
            widened,
            scaled,
            shifted,
            chan_scale,
            backward_activated,
        ) = backward_stored
        upstream_all = lax.all_gather(upstream.astype(jnp.bfloat16), "tp", axis=0, tiled=True)
        act_grad = jnp.einsum(
            "tbd,cd->tbc", upstream_all, project_weight[layer], preferred_element_type=jnp.float32
        )
        project_term = jnp.einsum(
            "tbc,tbd->cd", backward_activated, upstream_all, preferred_element_type=jnp.float32
        )
        sig_shift = jax.nn.sigmoid(shifted)
        shift_grad = act_grad * sig_shift * (1.0 + shifted * (1.0 - sig_shift)) * valid
        first_sum, cross_sum = lax.psum(
            (jnp.sum(shift_grad, axis=(0, 1)), jnp.sum(shift_grad * scaled, axis=(0, 1))), "ctx"
        )
        mixed_grad = (
            norm_gain[layer]
            * chan_scale
            * (shift_grad - first_sum / total - scaled * (cross_sum / total))
            * valid
        )
        wide_grad = padded(mixed_grad.astype(jnp.bfloat16), (("ctx", 0),), reach).astype(
            mixed_grad.dtype
        )
        tap_terms = jnp.stack(
            [
                jnp.sum(widened[offset : offset + frame_count] * mixed_grad, axis=(0, 1))
                for offset in range(2 * reach + 1)
            ]
        )
        tap_total = lax.psum(tap_terms, "ctx")
        taps = tap_weights[layer]
        glu_grad = taps[0] * wide_grad[2 * reach : 2 * reach + frame_count]
        for offset in range(1, 2 * reach + 1):
            glu_grad = (
                glu_grad
                + taps[offset] * wide_grad[2 * reach - offset : 2 * reach - offset + frame_count]
            )
        glu_grad = glu_grad * valid
        sig_gate = jax.nn.sigmoid(gate_pre)
        value_low = (glu_grad * sig_gate).astype(jnp.bfloat16)
        gate_low = (glu_grad * value_pre * sig_gate * (1.0 - sig_gate)).astype(jnp.bfloat16)
        value_term = jnp.einsum(
            "tbd,tbc->dc", gathered, value_low, preferred_element_type=jnp.float32
        )
        gate_term = jnp.einsum(
            "tbd,tbc->dc", gathered, gate_low, preferred_element_type=jnp.float32
        )
        normed_grad = lax.psum_scatter(
            (
                jnp.einsum(
                    "tbc,dc->tbd",
                    value_low,
                    value_weight[layer],
                    preferred_element_type=jnp.float32,
                )
                + jnp.einsum(
                    "tbc,dc->tbd", gate_low, gate_weight[layer], preferred_element_type=jnp.float32
                )
            ).astype(jnp.bfloat16),
            "tp",
            scatter_dimension=0,
            tiled=True,
        ).astype(jnp.float32)
        row_grad = ln_scale * (
            normed_grad
            - jnp.mean(normed_grad, axis=-1, keepdims=True)
            - normed * jnp.mean(normed_grad * normed, axis=-1, keepdims=True)
        )
        value_part = lax.psum_scatter(value_term, "ctx", scatter_dimension=0, tiled=True)
        gate_part = lax.psum_scatter(gate_term, "ctx", scatter_dimension=0, tiled=True)
        project_part = lax.psum_scatter(project_term, "ctx", scatter_dimension=1, tiled=True)
        upstream, value_part, gate_part, project_part, tap_total = (
            upstream + row_grad,
            value_part,
            gate_part,
            project_part,
            tap_total,
        )
        value_list.append(value_part)
        gate_list.append(gate_part)
        project_list.append(project_part)
        tap_list.append(tap_total)
    return (
        upstream,
        jnp.stack(value_list[::-1]),
        jnp.stack(gate_list[::-1]),
        jnp.stack(project_list[::-1]),
        jnp.stack(tap_list[::-1]),
    )


def solution(mesh):
    in_specs = (
        P(("ctx", "tp"), None, None),
        P(),
        P(None, None, "tp"),
        P(None, None, "tp"),
        P(None, None, "tp"),
        P(None, "tp"),
        P(None, "tp"),
        P(None, "tp", None),
        P(("ctx", "tp"), None, None),
    )
    out_specs = (
        P(("ctx", "tp"), None, None),
        P(None, "ctx", "tp"),
        P(None, "ctx", "tp"),
        P(None, "tp", "ctx"),
        P(None, None, "tp"),
    )
    return jax.shard_map(
        on_device, mesh=mesh, in_specs=in_specs, out_specs=out_specs, check_vma=False
    )
```

profile of v0, /device:TPU:1, one launch (start us, length us, event | category | flops | bytes accessed | tf_op | source)
XLA Modules:
  0.0 1706.8 jit_solution(949662380972403832)
XLA Ops:
  9.5 1.9 fusion.17
  16.3 1.5 fusion.138
  17.9 23.0 %all-gather.5.cloned.1.call-done = bf16[256,2,1024]{2,0,1:T(8,128)(2,1)} async-done(((bf16[64,2,1024]{2,0,1:T(8,128)(2,1)}), bf16[256,2,1024]{2,0,1:T(8,128)(2,1)}) %all-gather.5.cloned.1.call-update) | async-done | bytes 1048592 | tf_op jit(solution)/shard_map/all_gather | solution.py:51
  40.9 1.9 fusion.7
  44.1 4.6 collective-permute-start
  48.8 1.9 collective-permute-start.1
  54.0 2.9 multiply_reduce_fusion.67
  56.9 123.4 %psum.70 = f32[256]{0:T(256)S(1)} all-reduce(f32[256]{0:T(256)S(1)} %get-tuple-element.105), channel_id=1, replica_groups=mesh['ctx'=64,'tp'=4] {'ctx'}, use_global_device_ids=true, to_apply=%region_3.0 | all-reduce | flops 256 | bytes 2048 | tf_op jit(solution)/shard_map/psum | solution.py:68
  180.5 127.4 %psum.71 = f32[256]{0:T(256)S(1)} all-reduce(f32[256]{0:T(256)S(1)} %multiply_reduce_fusion.66), channel_id=1, replica_groups=mesh['ctx'=64,'tp'=4] {'ctx'}, use_global_device_ids=true, to_apply=%region_6.0 | all-reduce | flops 256 | bytes 2048 | tf_op jit(solution)/shard_map/psum | solution.py:69
  308.5 2.6 convolution_convert_fusion
  311.2 17.5 %reduce-scatter.10.cloned.1.call-done = bf16[64,2,1024]{2,0,1:T(8,128)(2,1)} async-done(((bf16[256,2,1024]{2,0,1:T(8,128)(2,1)}), bf16[64,2,1024]{2,0,1:T(8,128)(2,1)}) %reduce-scatter.10.cloned.1.call-update) | async-done | bytes 262160 | tf_op jit(solution)/shard_map/reduce_scatter | solution.py:92
  331.8 26.0 %all-gather.7.cloned.1.call-done = bf16[256,2,1024]{2,0,1:T(8,128)(2,1)} async-done(((bf16[64,2,1024]{2,0,1:T(8,128)(2,1)}), bf16[256,2,1024]{2,0,1:T(8,128)(2,1)}) %all-gather.7.cloned.1.call-update) | async-done | bytes 1048592 | tf_op jit(solution)/shard_map/all_gather | solution.py:51
  357.9 1.9 fusion.4
  359.9 2.3 multiply_convert_fusion.5
  362.2 4.6 collective-permute-start.2
  366.9 1.9 collective-permute-start.3
  369.9 2.0 collective-permute-done.3
  372.1 2.9 multiply_reduce_fusion.65
  375.2 122.8 %psum.72 = f32[256]{0:T(256)S(1)} all-reduce(f32[256]{0:T(256)S(1)} %get-tuple-element.101), channel_id=1, replica_groups=mesh['ctx'=64,'tp'=4] {'ctx'}, use_global_device_ids=true, to_apply=%region_11.12 | all-reduce | flops 256 | bytes 2048 | tf_op jit(solution)/shard_map/psum | solution.py:68
  499.2 127.0 %psum.73 = f32[256]{0:T(256)S(1)} all-reduce(f32[256]{0:T(256)S(1)} %multiply_reduce_fusion.64), channel_id=1, replica_groups=mesh['ctx'=64,'tp'=4] {'ctx'}, use_global_device_ids=true, to_apply=%region_13.14 | all-reduce | flops 256 | bytes 2048 | tf_op jit(solution)/shard_map/psum | solution.py:69
  626.3 2.9 fusion.126
  629.2 124.0 %all-reduce.2 = (f32[256]{0:T(256)S(1)}, f32[256]{0:T(256)S(1)}) all-reduce(f32[256]{0:T(256)S(1)} %get-tuple-element.80, f32[256]{0:T(256)S(1)} %get-tuple-element.79), channel_id=1, replica_groups=mesh['ctx'=64,'tp'=4] {'ctx'}, use_global_device_ids=true, to_apply=%region_17.18 | all-reduce | flops 512 | bytes 4096 | tf_op jit(solution)/shard_map/psum | solution.py:129
  753.3 3.0 multiply_reduce_fusion
  757.9 1.9 collective-permute-start.4
  759.8 2.6 collective-permute-start.5
  762.4 2.5 collective-permute-done.5
  765.2 2.2 multiply_convert_fusion.3
  770.4 17.4 %reduce-scatter.12.cloned.1.call-done = bf16[64,2,1024]{2,0,1:T(8,128)(2,1)} async-done(((bf16[256,2,1024]{2,0,1:T(8,128)(2,1)}), bf16[64,2,1024]{2,0,1:T(8,128)(2,1)}) %reduce-scatter.12.cloned.1.call-update) | async-done | bytes 262160 | tf_op jit(solution)/shard_map/reduce_scatter | solution.py:165
  789.0 1.9 fusion.123
  791.1 2.9 convolution_bitcast_fusion
  794.1 23.8 %all-gather.11.cloned.1.call-done = bf16[256,2,1024]{2,0,1:T(8,128)(2,1)} async-done(((bf16[64,2,1024]{2,0,1:T(8,128)(2,1)}), bf16[256,2,1024]{2,0,1:T(8,128)(2,1)}) %all-gather.11.cloned.1.call-update) | async-done | bytes 1048592 | tf_op jit(solution)/shard_map/all_gather | solution.py:120
  817.9 3.1 convolution_bitcast_fusion.1
  821.1 1.5 convolution_bitcast_fusion.2
  822.7 3.0 fusion.125
  825.7 125.6 %all-reduce.1 = (f32[256]{0:T(256)S(1)}, f32[256]{0:T(256)S(1)}) all-reduce(f32[256]{0:T(256)S(1)} %get-tuple-element.78, f32[256]{0:T(256)S(1)} %get-tuple-element.77), channel_id=1, replica_groups=mesh['ctx'=64,'tp'=4] {'ctx'}, use_global_device_ids=true, to_apply=%region_24.25 | all-reduce | flops 512 | bytes 4096 | tf_op jit(solution)/shard_map/psum | solution.py:129
  951.3 3.0 multiply_reduce_fusion.31
  955.8 2.0 collective-permute-start.6
  957.8 5.3 collective-permute-start.7
  964.1 3.0 multiply_convert_fusion.1
  968.6 2.4 convolution_bitcast_fusion.4
  976.7 1.5 add_convert_fusion
  978.7 2.9 stack.268
  981.5 241.1 %all-reduce = (f32[1,31,256]{2,1,0:T(8,128)S(1)}, f32[1,31,256]{2,1,0:T(8,128)S(1)}) all-reduce(f32[1,31,256]{2,1,0:T(8,128)S(1)} %bitcast.210, f32[1,31,256]{2,1,0:T(8,128)S(1)} %bitcast.211), channel_id=1, replica_groups=mesh['ctx'=64,'tp'=4] {'ctx'}, use_global_device_ids=true, to_apply=%region_97.98 | all-reduce | flops 15872 | bytes 126976 | tf_op jit(solution)/shard_map/psum | solution.py:147
  1224.7 16.3 reduce-scatter.22.cloned.1.call-done
  1240.9 141.6 %reduce-scatter.20.cloned.1.call-done = f32[16,256]{1,0:T(8,128)} async-done(((f32[1024,256]{1,0:T(8,128)}), f32[16,256]{1,0:T(8,128)}) %reduce-scatter.20.cloned.1.call-update) | async-done | bytes 16400 | tf_op jit(solution)/shard_map/reduce_scatter | solution.py:187
  1383.9 140.3 %reduce-scatter.18.cloned.1.call-done = f32[16,256]{1,0:T(8,128)} async-done(((f32[1024,256]{1,0:T(8,128)}), f32[16,256]{1,0:T(8,128)}) %reduce-scatter.18.cloned.1.call-update) | async-done | bytes 16400 | tf_op jit(solution)/shard_map/reduce_scatter | solution.py:186
  1524.2 141.6 %reduce-scatter.16.cloned.1.call-done = f32[16,256]{1,0:T(8,128)} async-done(((f32[1024,256]{1,0:T(8,128)}), f32[16,256]{1,0:T(8,128)}) %reduce-scatter.16.cloned.1.call-update) | async-done | bytes 16400 | tf_op jit(solution)/shard_map/reduce_scatter | solution.py:186
  1667.2 29.3 %reduce-scatter.14.cloned.1.call-done = bf16[64,2,1024]{2,0,1:T(8,128)(2,1)} async-done(((bf16[256,2,1024]{2,0,1:T(8,128)(2,1)}), bf16[64,2,1024]{2,0,1:T(8,128)(2,1)}) %reduce-scatter.14.cloned.1.call-update) | async-done | bytes 262160 | tf_op jit(solution)/shard_map/reduce_scatter | solution.py:165
  (408 shorter events, 41.0 us)
Async XLA Ops:
  7.2 33.7 %all-gather.5.cloned.1.call-start = ((), (), s32[]{:S(2)}) async-start(), calls=%async_computation.9 | async-start | bytes 1310720 | tf_op jit(solution)/shard_map/all_gather | solution.py:51
  11.4 317.3 %reduce-scatter.10.cloned.1.call-start = ((), (), s32[]{:S(2)}) async-start(), calls=%async_computation.10 | async-start | bytes 1310720 | tf_op jit(solution)/shard_map/reduce_scatter | solution.py:92
  17.8 36.1 %copy-start.22 = (f32[1,1,256]{2,0,1:T(1,128)}, f32[1,1,256]{2,0,1:T(1,128)S(1)}, u32[]{:S(2)}) copy-start(f32[1,1,256]{2,0,1:T(1,128)S(1)} %get-tuple-element.156) | copy-start | bytes 3076
  17.8 36.1 %copy-start.24 = (f32[1,1,256]{2,0,1:T(1,128)}, f32[1,1,256]{2,0,1:T(1,128)S(1)}, u32[]{:S(2)}) copy-start(f32[1,1,256]{2,0,1:T(1,128)S(1)} %get-tuple-element.157) | copy-start | bytes 3076
  17.9 36.1 %copy-start.26 = (f32[1,1,256]{2,0,1:T(1,128)}, f32[1,1,256]{2,0,1:T(1,128)S(1)}, u32[]{:S(2)}) copy-start(f32[1,1,256]{2,0,1:T(1,128)S(1)} %get-tuple-element.158) | copy-start | bytes 3076
  17.9 36.1 %copy-start.28 = (f32[1,1,256]{2,0,1:T(1,128)}, f32[1,1,256]{2,0,1:T(1,128)S(1)}, u32[]{:S(2)}) copy-start(f32[1,1,256]{2,0,1:T(1,128)S(1)} %get-tuple-element.159) | copy-start | bytes 3076
  17.9 25.0 %copy-start.9 = (bf16[2,1024,256]{2,1,0:T(8,128)(2,1)S(1)}, bf16[2,1024,256]{2,1,0:T(8,128)(2,1)}, u32[]{:S(2)}) copy-start(bf16[2,1024,256]{2,1,0:T(8,128)(2,1)} %param.11) | copy-start | bytes 3145732
  44.1 8.6 collective-permute-start
  48.8 5.1 collective-permute-start.1
  51.3 257.2 %copy-start.153 = (f32[1,256]{1,0:T(1,128)}, f32[1,256]{1,0:T(1,128)S(1)}, u32[]{:S(2)}) copy-start(f32[1,256]{1,0:T(1,128)S(1)} %get-tuple-element.182) | copy-start | bytes 3076
  53.9 253.9 %copy-start.149 = (f32[1,256]{1,0:T(1,128)S(1)}, f32[1,256]{1,0:T(1,128)}, u32[]{:S(2)}) copy-start(f32[1,256]{1,0:T(1,128)} %get-tuple-element.180) | copy-start | bytes 3076
  56.9 254.2 %copy-start.7 = (f32[256,2,256]{2,0,1:T(8,128)}, f32[256,2,256]{2,0,1:T(8,128)S(1)}, u32[]{:S(2)}) copy-start(f32[256,2,256]{2,0,1:T(8,128)S(1)} %get-tuple-element.106) | copy-start | bytes 1572868
  180.3 130.7 %copy-start.104 = (f32[256]{0:T(256)}, f32[256]{0:T(256)S(1)}, u32[]{:S(2)}) copy-start(f32[256]{0:T(256)S(1)} %broadcast_divide_fusion.5) | copy-start | bytes 3076
  308.5 20.2 %copy-start = (bf16[64,2,1024]{2,1,0:T(2,128)(2,1)S(1)}, bf16[64,2,1024]{2,1,0:T(2,128)(2,1)}, u32[]{:S(2)}) copy-start(bf16[64,2,1024]{2,1,0:T(2,128)(2,1)} %param.9) | copy-start | bytes 786436
  311.1 19.9 %copy-start.12 = (bf16[64,2,1024]{2,1,0:T(2,128)(2,1)S(1)}, bf16[64,2,1024]{2,1,0:T(2,128)(2,1)}, u32[]{:S(2)}) copy-start(bf16[64,2,1024]{2,1,0:T(2,128)(2,1)} %param.17) | copy-start | bytes 786436
  311.1 46.8 %all-gather.7.cloned.1.call-start = ((), (), s32[]{:S(2)}) async-start(), calls=%async_computation.11 | async-start | bytes 1310720 | tf_op jit(solution)/shard_map/all_gather | solution.py:51
  330.9 295.3 %all-gather.9.cloned.1.call-start = ((), (), s32[]{:S(2)}) async-start(), calls=%async_computation.12 | async-start | bytes 1310720 | tf_op jit(solution)/shard_map/all_gather | solution.py:120
  331.8 456.0 %reduce-scatter.12.cloned.1.call-start = ((), (), s32[]{:S(2)}) async-start(), calls=%async_computation.13 | async-start | bytes 1310720 | tf_op jit(solution)/shard_map/reduce_scatter | solution.py:165
  362.2 7.7 collective-permute-start.2
  366.9 5.1 collective-permute-start.3
  372.1 254.1 %copy-start.150 = (f32[1,256]{1,0:T(1,128)S(1)}, f32[1,256]{1,0:T(1,128)}, u32[]{:S(2)}) copy-start(f32[1,256]{1,0:T(1,128)} %get-tuple-element.179) | copy-start | bytes 3076
  372.1 254.2 %copy-start.154 = (f32[1,256]{1,0:T(1,128)S(1)}, f32[1,256]{1,0:T(1,128)}, u32[]{:S(2)}) copy-start(f32[1,256]{1,0:T(1,128)} %get-tuple-element.181) | copy-start | bytes 3076
  498.0 255.3 %copy-start.106 = (f32[256]{0:T(256)}, f32[256]{0:T(256)S(1)}, u32[]{:S(2)}) copy-start(f32[256]{0:T(256)S(1)} %broadcast_divide_fusion.4) | copy-start | bytes 3076
  626.3 127.0 %copy-start.147 = (f32[256]{0:T(256)}, f32[256]{0:T(256)S(1)}, u32[]{:S(2)}) copy-start(f32[256]{0:T(256)S(1)} %get-tuple-element.100) | copy-start | bytes 3076
  757.9 4.5 collective-permute-start.4
  759.8 5.1 collective-permute-start.5
  768.8 20.2 %copy-start.13 = (bf16[64,2,1024]{2,1,0:T(2,128)(2,1)S(1)}, bf16[64,2,1024]{2,1,0:T(2,128)(2,1)}, u32[]{:S(2)}) copy-start(bf16[64,2,1024]{2,1,0:T(2,128)(2,1)} %param.17) | copy-start | bytes 786436
  770.3 20.7 %copy-start.8 = (f32[256,2,256]{2,0,1:T(8,128)S(1)}, f32[256,2,256]{2,0,1:T(8,128)}, u32[]{:S(2)}) copy-start(f32[256,2,256]{2,0,1:T(8,128)} %get-tuple-element.102) | copy-start | bytes 1572868
  770.3 20.7 %copy-start.107 = (f32[256]{0:T(256)S(1)}, f32[256]{0:T(256)}, u32[]{:S(2)}) copy-start(f32[256]{0:T(256)} %copy-done.106) | copy-start | bytes 3076
  770.3 20.8 %copy-start.148 = (f32[256]{0:T(256)S(1)}, f32[256]{0:T(256)}, u32[]{:S(2)}) copy-start(f32[256]{0:T(256)} %copy-done.147) | copy-start | bytes 3076
  770.3 20.8 %copy-start.151 = (f32[1,256]{1,0:T(1,128)S(1)}, f32[1,256]{1,0:T(1,128)}, u32[]{:S(2)}) copy-start(f32[1,256]{1,0:T(1,128)} %get-tuple-element.179) | copy-start | bytes 3076
  770.3 20.8 %copy-start.155 = (f32[1,256]{1,0:T(1,128)S(1)}, f32[1,256]{1,0:T(1,128)}, u32[]{:S(2)}) copy-start(f32[1,256]{1,0:T(1,128)} %get-tuple-element.181) | copy-start | bytes 3076
  770.4 47.5 %all-gather.11.cloned.1.call-start = ((), (), s32[]{:S(2)}) async-start(), calls=%async_computation.14 | async-start | bytes 1310720 | tf_op jit(solution)/shard_map/all_gather | solution.py:120
  791.0 432.3 %reduce-scatter.26.cloned.1.call-start = ((), (), s32[]{:S(2)}) async-start(), calls=%async_computation.21 | async-start | bytes 1064960 | tf_op jit(solution)/shard_map/reduce_scatter | solution.py:188
  794.0 27.0 %copy-start.3 = (bf16[256,2,1024]{2,0,1:T(8,128)(2,1)S(1)}, bf16[256,2,1024]{2,0,1:T(8,128)(2,1)}, u32[]{:S(2)}) copy-start(bf16[256,2,1024]{2,0,1:T(8,128)(2,1)} %all-gather.7.cloned.1.call-done) | copy-start | bytes 3145732
  794.0 429.3 %reduce-scatter.24.cloned.1.call-start = ((), (), s32[]{:S(2)}) async-start(), calls=%async_computation.20 | async-start | bytes 1064960 | tf_op jit(solution)/shard_map/reduce_scatter | solution.py:188
  821.0 419.9 %reduce-scatter.22.cloned.1.call-start = ((), (), s32[]{:S(2)}) async-start(), calls=%async_computation.19 | async-start | bytes 1064960 | tf_op jit(solution)/shard_map/reduce_scatter | solution.py:187
  822.6 128.7 %copy-start.105 = (f32[256]{0:T(256)S(1)}, f32[256]{0:T(256)}, u32[]{:S(2)}) copy-start(f32[256]{0:T(256)} %copy-done.104) | copy-start | bytes 3076
  822.6 128.7 %copy-start.144 = (f32[256]{0:T(256)S(1)}, f32[256]{0:T(256)}, u32[]{:S(2)}) copy-start(f32[256]{0:T(256)} %get-tuple-element.95) | copy-start | bytes 3076
  822.6 128.7 %copy-start.146 = (f32[256]{0:T(256)S(1)}, f32[256]{0:T(256)}, u32[]{:S(2)}) copy-start(f32[256]{0:T(256)} %copy-done.145) | copy-start | bytes 3076
  822.6 559.9 %reduce-scatter.20.cloned.1.call-start = ((), (), s32[]{:S(2)}) async-start(), calls=%async_computation.18 | async-start | bytes 1064960 | tf_op jit(solution)/shard_map/reduce_scatter | solution.py:187
  955.8 7.2 collective-permute-start.6
  957.8 6.1 collective-permute-start.7
  968.6 555.7 %reduce-scatter.18.cloned.1.call-start = ((), (), s32[]{:S(2)}) async-start(), calls=%async_computation.17 | async-start | bytes 1064960 | tf_op jit(solution)/shard_map/reduce_scatter | solution.py:186
  971.1 694.8 %reduce-scatter.16.cloned.1.call-start = ((), (), s32[]{:S(2)}) async-start(), calls=%async_computation.16 | async-start | bytes 1064960 | tf_op jit(solution)/shard_map/reduce_scatter | solution.py:186
  974.5 721.9 %reduce-scatter.14.cloned.1.call-start = ((), (), s32[]{:S(2)}) async-start(), calls=%async_computation.15 | async-start | bytes 1310720 | tf_op jit(solution)/shard_map/reduce_scatter | solution.py:165
  978.2 719.5 %copy-start.14 = (bf16[64,2,1024]{2,1,0:T(2,128)(2,1)S(1)}, bf16[64,2,1024]{2,1,0:T(2,128)(2,1)}, u32[]{:S(2)}) copy-start(bf16[64,2,1024]{2,1,0:T(2,128)(2,1)} %param.17) | copy-start | bytes 786436
  978.2 719.5 %copy-start.15 = (bf16[64,2,1024]{2,0,1:T(8,128)(2,1)S(1)}, bf16[64,2,1024]{2,0,1:T(8,128)(2,1)}, u32[]{:S(2)}) copy-start(bf16[64,2,1024]{2,0,1:T(8,128)(2,1)} %reduce-scatter.12.cloned.1.call-done) | copy-start | bytes 786436
  (130 other events, 820.1 us)
Sparse Core Ops, SparseCore 0:
  11.5 29.3 all-gather.4
  311.2 17.3 reduce-scatter.9
  331.1 26.7 all-gather.6
  359.7 26.8 all-gather.8
  770.5 17.2 reduce-scatter.11
  791.1 26.7 all-gather.10
  821.9 135.7 reduce-scatter.25
  961.6 137.6 reduce-scatter.23
  1103.4 137.5 reduce-scatter.21
  1244.8 137.7 reduce-scatter.19
  1386.5 137.6 reduce-scatter.17
  1528.1 137.7 reduce-scatter.15
  1668.4 28.0 reduce-scatter.13
where the time goes:
time: 1710 us
  blocking collectives  991 us (58%)
  waiting for transfers between devices  584 us (34%)
  other arithmetic  40.7 us (2%)
  matrix products  33.6 us (2%)
  starting transfers between devices  25.6 us (1%)
    reduce_scatter x2, waiting for transfers between devices, on_device(): lax.psum_scatter(value_term, 'ctx', scatter_dimension=0, tiled=True)  282 us
    psum x2, blocking collectives, on_device(): lax.psum(jnp.sum(((mixed - chan_mean) * valid) ** 2, axis=(0, 1)), 'ctx')  254 us
    psum x2, blocking collectives, on_device(): lax.psum((jnp.sum(shift_grad, axis=(0, 1)), jnp.sum(shift_grad * scaled,...  250 us
    psum x2, blocking collectives, on_device(): chan_mean = lax.psum(jnp.sum(mixed * valid, axis=(0, 1)), 'ctx') / total  246 us
    psum x1, blocking collectives, on_device(): tap_total = lax.psum(tap_terms, 'ctx')  241 us
    reduce_scatter x2, waiting for transfers between devices, on_device(): lax.psum_scatter(gate_term, 'ctx', scatter_dimension=0, tiled=True)  158 us
    all_gather x2, waiting for transfers between devices, on_device(): forward_gathered = lax.all_gather(normed_low, 'tp', axis=0, tiled=True)  49.1 us
    reduce_scatter x2, waiting for transfers between devices, on_device(): lax.psum_scatter((jnp.einsum('tbc,dc->tbd', value_low, value_weight[layer...  46.7 us
  transfers between devices with their start and end apart: 21, of which 14 were waited for; matrix products, arithmetic and copies ran while one was open for 3% of the time, Pallas kernels for 0%

commit v1 on v0

v1 whole, which is shorter than its diff:
```python
import functools

import jax
import jax.numpy as jnp
from jax import lax
from jax.experimental import pallas as pl
from jax.experimental.pallas import tpu as pltpu
from jax.sharding import PartitionSpec as P

EPSILON = 1e-05
MESH = pl.DeviceIdType.MESH


def grid_of(ctx):
    return {64: (4, 8, 2), 8: (2, 2, 2), 4: (2, 1, 2)}[ctx]


def place(ctx):
    ny, nz, nc = grid_of(ctx)
    me = lax.axis_index("ctx")
    return me // (nz * nc), (me // nc) % nz, me % nc


def greet(peers):
    barrier = pltpu.get_barrier_semaphore()
    for peer in peers:
        pl.semaphore_signal(barrier, inc=1, device_id={"ctx": peer}, device_id_type=MESH)
    pl.semaphore_wait(barrier, len(peers))


def exchange(buf, me, count, target, send_sem, recv_sem):
    copies = []
    for step in range(1, count):
        peer = lax.rem(me + step, count)
        copy = pltpu.make_async_remote_copy(
            src_ref=buf.at[me],
            dst_ref=buf.at[me],
            send_sem=send_sem.at[step],
            recv_sem=recv_sem.at[me],
            device_id={"ctx": target(peer)},
            device_id_type=MESH,
        )
        copy.start()
        copies.append(copy)
    for step in range(1, count):
        peer = lax.rem(me + step, count)
        pltpu.make_async_remote_copy(
            src_ref=buf.at[peer],
            dst_ref=buf.at[peer],
            send_sem=send_sem.at[step],
            recv_sem=recv_sem.at[peer],
            device_id={"ctx": target(peer)},
            device_id_type=MESH,
        ).wait_recv()
    for copy in copies:
        copy.wait_send()


def merge_moments(buf, count):
    parts = [buf[i] for i in range(count)]
    num = parts[0][2:3]
    tot = parts[0][0:1]
    for p in parts[1:]:
        num = num + p[2:3]
        tot = tot + p[0:1]
    mean = tot / jnp.maximum(num, 1.0)
    square = jnp.zeros_like(mean)
    for p in parts:
        gap = p[0:1] / jnp.maximum(p[2:3], 1.0) - mean
        square = square + (p[1:2] + p[2:3] * gap * gap)
    return jnp.concatenate([tot, square, num, jnp.zeros_like(parts[0][3:])], axis=0)


def merge_sum(buf, count):
    total = buf[0]
    for i in range(1, count):
        total = total + buf[i]
    return total


def reduce_kernel(ctx, merge, x_ref, o_ref, first, second, send1, recv1, send2, recv2):
    ny, nz, nc = grid_of(ctx)
    y, z, c = place(ctx)
    one = lambda p: ((p // nc) * nz + z) * nc + p % nc
    two = lambda p: (y * nz + p) * nc + c
    mine = y * nc + c
    greet(
        [one(lax.rem(mine + s, ny * nc)) for s in range(1, ny * nc)]
        + [two(lax.rem(z + s, nz)) for s in range(1, nz)]
    )
    first[mine] = x_ref[...]
    exchange(first, mine, ny * nc, one, send1, recv1)
    second[z] = merge(first, ny * nc)
    exchange(second, z, nz, two, send2, recv2)
    o_ref[...] = merge(second, nz)


def all_reduce(x, merge, cid):
    ctx = lax.axis_size("ctx")
    ny, nz, nc = grid_of(ctx)
    return pl.pallas_call(
        functools.partial(reduce_kernel, ctx, merge),
        out_shape=jax.ShapeDtypeStruct(x.shape, x.dtype),
        in_specs=[pl.BlockSpec(memory_space=pltpu.VMEM)],
        out_specs=pl.BlockSpec(memory_space=pltpu.VMEM),
        scratch_shapes=[
            pltpu.VMEM((ny * nc,) + x.shape, x.dtype),
            pltpu.VMEM((nz,) + x.shape, x.dtype),
            pltpu.SemaphoreType.DMA((ny * nc,)),
            pltpu.SemaphoreType.DMA((ny * nc,)),
            pltpu.SemaphoreType.DMA((nz,)),
            pltpu.SemaphoreType.DMA((nz,)),
        ],
        compiler_params=pltpu.CompilerParams(collective_id=cid, has_side_effects=True),
    )(x)


def scatter_kernel(ctx, x_ref, o_ref, in1, in2, in3, out2, out3, ssem, rsem):
    ny, nz, nc = grid_of(ctx)
    y, z, c = place(ctx)
    k = x_ref.shape[0]
    ids_c = [((y * nz + z) * nc + lax.rem(c + s, nc)) for s in range(1, nc)]
    ids_y = [((lax.rem(y + s, ny) * nz + z) * nc + c) for s in range(1, ny)]
    ids_z = [((y * nz + lax.rem(z + s, nz)) * nc + c) for s in range(1, nz)]
    greet(ids_c + ids_y + ids_z)

    def send(src, dst, sem, target):
        copy = pltpu.make_async_remote_copy(
            src_ref=src,
            dst_ref=dst,
            send_sem=ssem.at[sem],
            recv_sem=rsem.at[sem],
            device_id={"ctx": target},
            device_id_type=MESH,
        )
        copy.start()
        return copy

    other = lax.rem(c + 1, nc)
    copy = send(x_ref.at[:, :, :, other], in1, 0, ids_c[0])
    copy.wait()

    def add1(i, carry):
        a, b = i // (ny * nz), i % (ny * nz)
        iy, iz = b // nz, b % nz
        out2[a, iy, iz] = (
            x_ref[a, iy, iz, c].astype(jnp.float32) + in1[a, iy, iz].astype(jnp.float32)
        ).astype(jnp.bfloat16)
        return carry

    lax.fori_loop(0, k * ny * nz, add1, 0)
    copies = []
    for s in range(1, ny):
        copies.append(send(out2.at[:, lax.rem(y + s, ny)], in2.at[s - 1], s, ids_y[s - 1]))
    for copy in copies:
        copy.wait()

    def add2(i, carry):
        a, iz = i // nz, i % nz
        total = out2[a, y, iz].astype(jnp.float32)
        for s in range(ny - 1):
            total = total + in2[s, a, iz].astype(jnp.float32)
        out3[a, iz] = total.astype(jnp.bfloat16)
        return carry

    lax.fori_loop(0, k * nz, add2, 0)
    copies = []
    for s in range(1, nz):
        copies.append(send(out3.at[:, lax.rem(z + s, nz)], in3.at[s - 1], ny + s, ids_z[s - 1]))
    for copy in copies:
        copy.wait()

    def add3(a, carry):
        total = out3[a, z].astype(jnp.float32)
        for s in range(nz - 1):
            total = total + in3[s, a].astype(jnp.float32)
        o_ref[a] = total
        return carry

    lax.fori_loop(0, k, add3, 0)


def scatter_rows(x, cid):
    ctx = lax.axis_size("ctx")
    ny, nz, nc = grid_of(ctx)
    k, rows, width = x.shape
    piece = rows // ctx
    x = x.reshape(k, ny, nz, nc, piece, width)
    return pl.pallas_call(
        functools.partial(scatter_kernel, ctx),
        out_shape=jax.ShapeDtypeStruct((k, piece, width), jnp.float32),
        in_specs=[pl.BlockSpec(memory_space=pltpu.VMEM)],
        out_specs=pl.BlockSpec(memory_space=pltpu.VMEM),
        scratch_shapes=[
            pltpu.VMEM((k, ny, nz, piece, width), x.dtype),
            pltpu.VMEM((ny - 1, k, nz, piece, width), x.dtype),
            pltpu.VMEM((max(nz - 1, 1), k, piece, width), x.dtype),
            pltpu.VMEM((k, ny, nz, piece, width), x.dtype),
            pltpu.VMEM((k, nz, piece, width), x.dtype),
            pltpu.SemaphoreType.DMA((ny + nz,)),
            pltpu.SemaphoreType.DMA((ny + nz,)),
        ],
        compiler_params=pltpu.CompilerParams(
            collective_id=cid, has_side_effects=True, vmem_limit_bytes=40 * 1024 * 1024
        ),
    )(x)


def padded(block, sides, width):
    for axis, dim in sides:
        count = lax.axis_size(axis)
        forward = [(i, i + 1) for i in range(count - 1)]
        backward = [(target, source) for source, target in forward]
        low = lax.ppermute(
            lax.slice_in_dim(block, block.shape[dim] - width, None, axis=dim), axis, forward
        )
        high = lax.ppermute(lax.slice_in_dim(block, 0, width, axis=dim), axis, backward)
        block = jnp.concatenate([low, block, high], axis=dim)
    return block


def on_device(
    frames,
    lengths,
    value_weight,
    gate_weight,
    tap_weights,
    norm_gain,
    norm_shift,
    project_weight,
    output_grad,
):
    local_rows = frames.shape[0]
    frame_count = local_rows * lax.axis_size("tp")
    reach = tap_weights.shape[1] // 2
    layer_count = value_weight.shape[0]
    width = tap_weights.shape[2]
    first_frame = lax.axis_index("ctx") * frame_count
    positions = first_frame + jnp.arange(frame_count, dtype=jnp.int32)[:, None]
    valid = (positions < lengths[None, :]).astype(jnp.float32)[:, :, None]
    total = jnp.sum(lengths).astype(jnp.float32)
    local_count = jnp.sum(jnp.clip(lengths - first_frame, 0, frame_count)).astype(jnp.float32)
    stored_list = []
    hidden = frames
    for layer in range(layer_count):
        rows32 = hidden.astype(jnp.float32)
        centered = rows32 - jnp.mean(rows32, axis=-1, keepdims=True)
        ln_scale = lax.rsqrt(jnp.mean(centered * centered, axis=-1, keepdims=True) + EPSILON)
        normed = centered * ln_scale
        normed_low = normed.astype(jnp.bfloat16)
        gathered = lax.all_gather(normed_low, "tp", axis=0, tiled=True)
        value_pre = jnp.einsum(
            "tbd,dc->tbc", gathered, value_weight[layer], preferred_element_type=jnp.float32
        )
        gate_pre = jnp.einsum(
            "tbd,dc->tbc", gathered, gate_weight[layer], preferred_element_type=jnp.float32
        )
        glu = (value_pre * jax.nn.sigmoid(gate_pre) * valid).astype(jnp.bfloat16)
        widened = padded(glu, (("ctx", 0),), reach).astype(jnp.float32)
        taps = tap_weights[layer]
        mixed = taps[0] * widened[0:frame_count]
        for offset in range(1, 2 * reach + 1):
            mixed = mixed + taps[offset] * widened[offset : offset + frame_count]
        local_sum = jnp.sum(mixed * valid, axis=(0, 1))
        local_mean = local_sum / jnp.maximum(local_count, 1.0)
        local_square = jnp.sum(((mixed - local_mean) * valid) ** 2, axis=(0, 1))
        moments = jnp.concatenate(
            [
                local_sum[None],
                local_square[None],
                jnp.full((1, width), local_count),
                jnp.zeros((5, width), jnp.float32),
            ]
        )
        moments = all_reduce(moments, merge_moments, 0)
        chan_mean = moments[0] / total
        chan_var = moments[1] / total
        chan_scale = lax.rsqrt(chan_var + EPSILON)
        scaled = (mixed - chan_mean) * chan_scale
        shifted = norm_gain[layer] * scaled + norm_shift[layer]
        activated = (jax.nn.silu(shifted) * valid).astype(jnp.bfloat16)
        stored_list.append(
            (
                normed,
                ln_scale,
                gathered,
                value_pre,
                gate_pre,
                widened,
                scaled,
                shifted,
                chan_scale,
                activated,
            )
        )
        if layer + 1 < layer_count:
            branch = lax.psum_scatter(
                jnp.einsum(
                    "tbc,cd->tbd",
                    activated,
                    project_weight[layer],
                    preferred_element_type=jnp.float32,
                ).astype(jnp.bfloat16),
                "tp",
                scatter_dimension=0,
                tiled=True,
            ).astype(jnp.float32)
            hidden = (rows32 + branch).astype(jnp.bfloat16)
    upstream = output_grad.astype(jnp.float32)
    weight_terms = [None] * (3 * layer_count)
    tap_list = [None] * layer_count
    for layer in range(layer_count - 1, -1, -1):
        (
            normed,
            ln_scale,
            gathered,
            value_pre,
            gate_pre,
            widened,
            scaled,
            shifted,
            chan_scale,
            activated,
        ) = stored_list[layer]
        upstream_all = lax.all_gather(upstream.astype(jnp.bfloat16), "tp", axis=0, tiled=True)
        act_grad = jnp.einsum(
            "tbd,cd->tbc", upstream_all, project_weight[layer], preferred_element_type=jnp.float32
        )
        weight_terms[3 * layer + 2] = jnp.einsum(
            "tbd,tbc->dc", upstream_all, activated, preferred_element_type=jnp.float32
        ).astype(jnp.bfloat16)
        sig_shift = jax.nn.sigmoid(shifted)
        shift_grad = act_grad * sig_shift * (1.0 + shifted * (1.0 - sig_shift)) * valid
        sums = jnp.concatenate(
            [
                jnp.sum(shift_grad, axis=(0, 1))[None],
                jnp.sum(shift_grad * scaled, axis=(0, 1))[None],
                jnp.zeros((6, width), jnp.float32),
            ]
        )
        sums = all_reduce(sums, merge_sum, 1)
        mixed_grad = (
            norm_gain[layer]
            * chan_scale
            * (shift_grad - sums[0] / total - scaled * (sums[1] / total))
            * valid
        )
        wide_grad = padded(mixed_grad.astype(jnp.bfloat16), (("ctx", 0),), reach).astype(
            mixed_grad.dtype
        )
        tap_list[layer] = jnp.stack(
            [
                jnp.sum(widened[offset : offset + frame_count] * mixed_grad, axis=(0, 1))
                for offset in range(2 * reach + 1)
            ]
            + [jnp.zeros((width,), jnp.float32)]
        )
        taps = tap_weights[layer]
        glu_grad = taps[0] * wide_grad[2 * reach : 2 * reach + frame_count]
        for offset in range(1, 2 * reach + 1):
            glu_grad = (
                glu_grad
                + taps[offset] * wide_grad[2 * reach - offset : 2 * reach - offset + frame_count]
            )
        glu_grad = glu_grad * valid
        sig_gate = jax.nn.sigmoid(gate_pre)
        value_low = (glu_grad * sig_gate).astype(jnp.bfloat16)
        gate_low = (glu_grad * value_pre * sig_gate * (1.0 - sig_gate)).astype(jnp.bfloat16)
        weight_terms[3 * layer] = jnp.einsum(
            "tbd,tbc->dc", gathered, value_low, preferred_element_type=jnp.float32
        ).astype(jnp.bfloat16)
        weight_terms[3 * layer + 1] = jnp.einsum(
            "tbd,tbc->dc", gathered, gate_low, preferred_element_type=jnp.float32
        ).astype(jnp.bfloat16)
        normed_grad = lax.psum_scatter(
            (
                jnp.einsum(
                    "tbc,dc->tbd",
                    value_low,
                    value_weight[layer],
                    preferred_element_type=jnp.float32,
                )
                + jnp.einsum(
                    "tbc,dc->tbd", gate_low, gate_weight[layer], preferred_element_type=jnp.float32
                )
            ).astype(jnp.bfloat16),
            "tp",
            scatter_dimension=0,
            tiled=True,
        ).astype(jnp.float32)
        row_grad = ln_scale * (
            normed_grad
            - jnp.mean(normed_grad, axis=-1, keepdims=True)
            - normed * jnp.mean(normed_grad * normed, axis=-1, keepdims=True)
        )
        upstream = upstream + row_grad
    parts = scatter_rows(jnp.stack(weight_terms), 2)
    parts = parts.reshape((layer_count, 3) + parts.shape[1:])
    tap_all = all_reduce(jnp.concatenate(tap_list), merge_sum, 3)
    tap_all = tap_all.reshape(layer_count, -1, width)[:, : 2 * reach + 1]
    return (
        upstream,
        parts[:, 0],
        parts[:, 1],
        jnp.swapaxes(parts[:, 2], 1, 2),
        tap_all,
    )


def solution(mesh):
    in_specs = (
        P(("ctx", "tp"), None, None),
        P(),
        P(None, None, "tp"),
        P(None, None, "tp"),
        P(None, None, "tp"),
        P(None, "tp"),
        P(None, "tp"),
        P(None, "tp", None),
        P(("ctx", "tp"), None, None),
    )
    out_specs = (
        P(("ctx", "tp"), None, None),
        P(None, "ctx", "tp"),
        P(None, "ctx", "tp"),
        P(None, "tp", "ctx"),
        P(None, None, "tp"),
    )
    return jax.shard_map(
        on_device, mesh=mesh, in_specs=in_specs, out_specs=out_specs, check_vma=False
    )
```

time: 1710 us -> 396 us (0.23)
  blocking collectives: 991 us -> 0 us
  waiting for transfers between devices: 584 us -> 124 us
  Pallas kernels: 0 us -> 131 us
    psum x7 -> x0, blocking collectives: 991 us -> none  [the longest x2 254 us: on_device(): lax.psum(jnp.sum(((mixed - chan_mean) * valid) ** 2, axis=(0, 1)), 'ctx')]
    reduce_scatter x6 -> x0, waiting for transfers between devices: 440 us -> none  [the longest x2 282 us: on_device(): lax.psum_scatter(value_term, 'ctx', scatter_dimension=0, tiled=True)]
    pallas_call x0 -> x6, Pallas kernels: none -> 131 us  [the longest x5 90.3 us: all_reduce(): pl.pallas_call(functools.partial(reduce_kernel, ctx, merge), out_shape=ja...]
    reduce_scatter x2, waiting for transfers between devices: 46.7 us -> 22.3 us  [on_device(): lax.psum_scatter((jnp.einsum('tbc,dc->tbd', value_low, value_weight[layer...]
  transfers between devices with their start and end apart: 21 -> 15, of which waited for: 14 -> 9; matrix products, arithmetic and copies ran while one was open for 3% -> 11% of each run, Pallas kernels for 0% -> 22%
where the time goes in v1:
time: 396 us; the launch traced here: 394 us
  Pallas kernels  131 us (33%)
  waiting for transfers between devices  124 us (31%)
  other arithmetic  42.2 us (11%)
  matrix products  27.3 us (7%)
  local copies, waits for them, and re-layouts  25.7 us (6%)
  starting transfers between devices  25.5 us (6%)
  between operations  17.7 us (4%)
    pallas_call x5, Pallas kernels, all_reduce(): pl.pallas_call(functools.partial(reduce_kernel, ctx, merge), out_shape=ja...  90.3 us
    all_gather x2, waiting for transfers between devices, on_device(): gathered = lax.all_gather(normed_low, 'tp', axis=0, tiled=True)  47.5 us
    pallas_call x1, Pallas kernels, scatter_rows(): pl.pallas_call(functools.partial(scatter_kernel, ctx), out_shape=jax.Shap...  40.5 us
    all_gather x2, waiting for transfers between devices, on_device(): lax.all_gather(upstream.astype(jnp.bfloat16), 'tp', axis=0, tiled=True)  26.8 us
    reduce_scatter x2, waiting for transfers between devices, on_device(): lax.psum_scatter((jnp.einsum('tbc,dc->tbd', value_low, value_weight[layer...  22.3 us
    reduce_scatter x1, waiting for transfers between devices, on_device(): lax.psum_scatter(jnp.einsum('tbc,cd->tbd', activated, project_weight[laye...  22.1 us
    ppermute x4, starting transfers between devices, padded(): lax.ppermute(lax.slice_in_dim(block, block.shape[dim] - width, None, axis...  17 us
    concatenate x1, local copies, waits for them, and re-layouts, on_device(): tap_all = all_reduce(jnp.concatenate(tap_list), merge_sum, 3)  8.4 us
  transfers between devices with their start and end apart: 15, of which 9 were waited for; matrix products, arithmetic and copies ran while one was open for 11% of the time, Pallas kernels for 22%

profile of v1, /device:TPU:1, one launch (start us, length us, event | category | flops | bytes accessed | tf_op | source)
XLA Modules:
  0.0 393.7 jit_solution(5948293929990613685)
XLA Ops:
  9.6 1.9 fusion.24
  12.3 1.4 fusion.146
  16.3 1.5 fusion.143
  17.8 1.5 fusion.144
  19.4 21.6 %all-gather.5.cloned.1.call-done = bf16[256,2,1024]{2,0,1:T(8,128)(2,1)} async-done(((bf16[64,2,1024]{2,0,1:T(8,128)(2,1)}), bf16[256,2,1024]{2,0,1:T(8,128)(2,1)}) %all-gather.5.cloned.1.call-update) | async-done | bytes 1048592 | tf_op jit(solution)/shard_map/all_gather | solution.py:251
  41.0 1.9 fusion.14
  44.2 4.6 %collective-permute-start = (bf16[15,2,256]{2,0,1:T(8,128)(2,1)S(1)}, bf16[15,2,256]{2,0,1:T(8,128)(2,1)S(1)}, u32[]{:S(2)}, u32[]{:S(2)}) collective-permute-start(bf16[15,2,256]{2,0,1:T(8,128)(2,1)S(1)} %get-tuple-element.102), channel_id=1, source_target_pairs={{0,4},{4,8},{8,12},{12,16},{16,20},{20,24},{24,28},{28,32},{32,36}... | collective-permute-start | bytes 46088 | tf_op jit(solution)/shard_map/ppermute | solution.py:214
  48.8 1.9 collective-permute-start.1
  54.0 3.1 multiply_reduce_fusion.67
  57.9 15.8 %shard_map.128 = f32[8,256]{1,0:T(8,128)} custom-call(f32[8,256]{1,0:T(8,128)} %maximum_maximum_fusion.x_ref), custom_call_target="tpu_custom_call" | custom-call | tf_op jit(solution)/shard_map/pallas_call | solution.py:101
  74.5 2.6 convolution_convert_fusion
  77.3 22.1 %reduce-scatter.4.cloned.1.call-done = bf16[64,2,1024]{2,0,1:T(8,128)(2,1)} async-done(((bf16[256,2,1024]{2,0,1:T(8,128)(2,1)}), bf16[64,2,1024]{2,0,1:T(8,128)(2,1)}) %reduce-scatter.4.cloned.1.call-update) | async-done | bytes 262160 | tf_op jit(solution)/shard_map/reduce_scatter | solution.py:297
  102.5 25.9 %all-gather.7.cloned.1.call-done = bf16[256,2,1024]{2,0,1:T(8,128)(2,1)} async-done(((bf16[64,2,1024]{2,0,1:T(8,128)(2,1)}), bf16[256,2,1024]{2,0,1:T(8,128)(2,1)}) %all-gather.7.cloned.1.call-update) | async-done | bytes 1048592 | tf_op jit(solution)/shard_map/all_gather | solution.py:251
  128.4 1.9 fusion.11
  131.6 4.6 %collective-permute-start.2 = (bf16[15,2,256]{2,0,1:T(8,128)(2,1)S(1)}, bf16[15,2,256]{2,0,1:T(8,128)(2,1)S(1)}, u32[]{:S(2)}, u32[]{:S(2)}) collective-permute-start(bf16[15,2,256]{2,0,1:T(8,128)(2,1)S(1)} %get-tuple-element.100), channel_id=1, source_target_pairs={{0,4},{4,8},{8,12},{12,16},{16,20},{20,24},{24,28},{28,32},{32,36}... | collective-permute-start | bytes 46088 | tf_op jit(solution)/shard_map/ppermute | solution.py:214
  136.3 1.9 collective-permute-start.3
  139.9 1.4 collective-permute-done.3
  141.4 2.9 multiply_reduce_fusion.65
  145.4 15.8 %shard_map.129 = f32[8,256]{1,0:T(8,128)} custom-call(f32[8,256]{1,0:T(8,128)} %maximum_maximum_fusion.1.x_ref), custom_call_target="tpu_custom_call" | custom-call | tf_op jit(solution)/shard_map/pallas_call | solution.py:101
  161.2 1.4 slice_divide_fusion.4
  164.4 2.8 fusion.133
  168.5 12.8 %shard_map.130 = f32[8,256]{1,0:T(8,128)} custom-call(f32[8,256]{1,0:T(8,128)} %maximum_maximum_fusion.2.x_ref), custom_call_target="tpu_custom_call" | custom-call | tf_op jit(solution)/shard_map/pallas_call | solution.py:101
  182.1 2.8 multiply_reduce_fusion
  185.2 1.4 multiply_reduce_fusion.18
  186.6 4.4 %collective-permute-start.4 = (bf16[15,2,256]{2,0,1:T(8,128)(2,1)S(1)}, bf16[15,2,256]{2,0,1:T(8,128)(2,1)S(1)}, u32[]{:S(2)}, u32[]{:S(2)}) collective-permute-start(bf16[15,2,256]{2,0,1:T(8,128)(2,1)S(1)} %get-tuple-element.98), channel_id=1, source_target_pairs={{0,4},{4,8},{8,12},{12,16},{16,20},{20,24},{24,28},{28,32},{32,36}... | collective-permute-start | bytes 46088 | tf_op jit(solution)/shard_map/ppermute | solution.py:214
  191.0 2.1 collective-permute-start.5
  193.2 2.9 collective-permute-done.5
  196.5 2.2 multiply_convert_fusion.3
  200.2 1.5 add_convert_fusion.1
  201.7 22.3 %reduce-scatter.6.cloned.1.call-done = bf16[64,2,1024]{2,0,1:T(8,128)(2,1)} async-done(((bf16[256,2,1024]{2,0,1:T(8,128)(2,1)}), bf16[64,2,1024]{2,0,1:T(8,128)(2,1)}) %reduce-scatter.6.cloned.1.call-update) | async-done | bytes 262160 | tf_op jit(solution)/shard_map/reduce_scatter | solution.py:375
  225.3 1.9 fusion.130
  227.3 26.8 %all-gather.11.cloned.1.call-done = bf16[256,2,1024]{2,0,1:T(8,128)(2,1)} async-done(((bf16[64,2,1024]{2,0,1:T(8,128)(2,1)}), bf16[256,2,1024]{2,0,1:T(8,128)(2,1)}) %all-gather.11.cloned.1.call-update) | async-done | bytes 1048592 | tf_op jit(solution)/shard_map/all_gather | solution.py:325
  254.1 2.0 fusion.132
  256.8 16.1 %shard_map.131 = f32[8,256]{1,0:T(8,128)} custom-call(f32[8,256]{1,0:T(8,128)} %maximum_maximum_fusion.3.x_ref), custom_call_target="tpu_custom_call" | custom-call | tf_op jit(solution)/shard_map/pallas_call | solution.py:101
  273.7 1.7 multiply_reduce_fusion.31
  275.4 1.4 multiply_reduce_fusion.49
  276.8 3.3 collective-permute-start.6
  280.3 2.3 collective-permute-start.7
  286.6 3.1 multiply_convert_fusion.1
  291.0 1.5 add_convert_fusion
  292.8 2.5 fusion.3
  295.3 1.7 fusion.4
  297.3 8.4 %concatenate.36.x_ref = f32[64,256]{1,0:T(8,128)} concatenate(f32[1,256]{1,0:T(1,128)} %bitcast.462, f32[1,256]{1,0:T(1,128)} %bitcast.461, f32[1,256]{1,0:T(1,128)} %bitcast.460, f32[1,256]{1,0:T(1,128)} %bitcast.459, f32[1,256]{1,0:T(1,128)} %bitcast.458, f32[1,256]{1,0:T(1,128)} %bitcast.457, f32[1,256]{1,0:T(1,128)} %bitcast.456, f32[1,256]{1,0:T(1,128)} %bitcast.455, ...), dimensions={0} | concatenate | bytes 131072 | tf_op jit(solution)/shard_map/concatenate | solution.py:399
  305.7 29.8 %shard_map.133 = f32[64,256]{1,0:T(8,128)} custom-call(f32[64,256]{1,0:T(8,128)} %concatenate.36.x_ref), custom_call_target="tpu_custom_call" | custom-call | tf_op jit(solution)/shard_map/pallas_call | solution.py:101
  335.6 1.5 copy.28
  337.1 1.9 fusion.2
  339.0 1.7 fusion
  341.9 40.5 %shard_map.132 = f32[6,16,256]{2,1,0:T(8,128)S(1)} custom-call(bf16[6,4,8,2,16,256]{5,4,3,2,1,0:T(8,128)(2,1)S(1)} %constant_dynamic-update-slice_fusion.x_ref), custom_call_target="tpu_custom_call" | custom-call | tf_op jit(solution)/shard_map/pallas_call | solution.py:189
  (366 shorter events, 36.7 us)
Async XLA Ops:
  7.2 35.8 %copy-start.3 = (bf16[2,1024,256]{2,1,0:T(8,128)(2,1)S(1)}, bf16[2,1024,256]{2,1,0:T(8,128)(2,1)}, u32[]{:S(2)}) copy-start(bf16[2,1024,256]{2,1,0:T(8,128)(2,1)} %param.11) | copy-start | bytes 3145732
  7.2 33.8 %all-gather.5.cloned.1.call-start = ((), (), s32[]{:S(2)}) async-start(), calls=%async_computation.3 | async-start | bytes 1310720 | tf_op jit(solution)/shard_map/all_gather | solution.py:251
  9.6 34.6 %copy-start.21 = (f32[64,2]{0,1:T(2,128)}, f32[64,2]{0,1:T(2,128)S(1)}, u32[]{:S(2)}) copy-start(f32[64,2]{0,1:T(2,128)S(1)} %add_rsqrt_fusion.3) | copy-start | bytes 1540
  11.5 87.9 %reduce-scatter.4.cloned.1.call-start = ((), (), s32[]{:S(2)}) async-start(), calls=%async_computation.4 | async-start | bytes 1310720 | tf_op jit(solution)/shard_map/reduce_scatter | solution.py:297
  16.3 37.7 %copy-start.23 = (f32[1,1,256]{2,0,1:T(1,128)}, f32[1,1,256]{2,0,1:T(1,128)S(1)}, u32[]{:S(2)}) copy-start(f32[1,1,256]{2,0,1:T(1,128)S(1)} %get-tuple-element.165) | copy-start | bytes 3076
  16.3 37.7 %copy-start.25 = (f32[1,1,256]{2,0,1:T(1,128)}, f32[1,1,256]{2,0,1:T(1,128)S(1)}, u32[]{:S(2)}) copy-start(f32[1,1,256]{2,0,1:T(1,128)S(1)} %get-tuple-element.166) | copy-start | bytes 3076
  19.4 31.4 %copy-start.133 = (s32[2]{0:T(128)S(1)}, s32[2]{0:T(128)}, u32[]{:S(2)}) copy-start(s32[2]{0:T(128)} %param.10) | copy-start | bytes 28
  44.2 8.7 %collective-permute-start = (bf16[15,2,256]{2,0,1:T(8,128)(2,1)S(1)}, bf16[15,2,256]{2,0,1:T(8,128)(2,1)S(1)}, u32[]{:S(2)}, u32[]{:S(2)}) collective-permute-start(bf16[15,2,256]{2,0,1:T(8,128)(2,1)S(1)} %get-tuple-element.102), channel_id=1, source_target_pairs={{0,4},{4,8},{8,12},{12,16},{16,20},{20,24},{24,28},{28,32},{32,36}... | collective-permute-start | bytes 46088 | tf_op jit(solution)/shard_map/ppermute | solution.py:214
  48.8 5.1 %collective-permute-start.1 = (bf16[15,2,256]{2,0,1:T(8,128)(2,1)S(1)}, bf16[15,2,256]{2,0,1:T(8,128)(2,1)S(1)}, u32[]{:S(2)}, u32[]{:S(2)}) collective-permute-start(bf16[15,2,256]{2,0,1:T(8,128)(2,1)S(1)} %get-tuple-element.103), channel_id=1, source_target_pairs={{4,0},{8,4},{12,8},{16,12},{20,16},{24,20},{28,24},{32,28},{36,32}... | collective-permute-start | bytes 46088 | tf_op jit(solution)/shard_map/ppermute | solution.py:217
  54.0 20.5 %copy-start.126 = (f32[1,256]{1,0:T(1,128)S(1)}, f32[1,256]{1,0:T(1,128)}, u32[]{:S(2)}) copy-start(f32[1,256]{1,0:T(1,128)} %get-tuple-element.178) | copy-start | bytes 3076
  54.0 20.5 %copy-start.135 = (f32[1,256]{1,0:T(1,128)S(1)}, f32[1,256]{1,0:T(1,128)}, u32[]{:S(2)}) copy-start(f32[1,256]{1,0:T(1,128)} %get-tuple-element.180) | copy-start | bytes 3076
  57.1 42.3 %copy-start = (bf16[64,2,1024]{2,1,0:T(2,128)(2,1)S(1)}, bf16[64,2,1024]{2,1,0:T(2,128)(2,1)}, u32[]{:S(2)}) copy-start(bf16[64,2,1024]{2,1,0:T(2,128)(2,1)} %param.9) | copy-start | bytes 786436
  74.5 26.0 %copy-start.89 = (f32[1,256]{1,0:T(1,128)}, f32[1,256]{1,0:T(1,128)S(1)}, u32[]{:S(2)}) copy-start(f32[1,256]{1,0:T(1,128)S(1)} %get-tuple-element.176) | copy-start | bytes 3076
  74.5 27.2 %copy-start.6 = (bf16[64,2,1024]{2,1,0:T(2,128)(2,1)S(1)}, bf16[64,2,1024]{2,1,0:T(2,128)(2,1)}, u32[]{:S(2)}) copy-start(bf16[64,2,1024]{2,1,0:T(2,128)(2,1)} %param.17) | copy-start | bytes 786436
  77.2 51.2 %all-gather.7.cloned.1.call-start = ((), (), s32[]{:S(2)}) async-start(), calls=%async_computation.5 | async-start | bytes 1310720 | tf_op jit(solution)/shard_map/all_gather | solution.py:251
  101.7 62.7 %all-gather.9.cloned.1.call-start = ((), (), s32[]{:S(2)}) async-start(), calls=%async_computation.6 | async-start | bytes 1310720 | tf_op jit(solution)/shard_map/all_gather | solution.py:325
  102.5 121.6 %reduce-scatter.6.cloned.1.call-start = ((), (), s32[]{:S(2)}) async-start(), calls=%async_computation.7 | async-start | bytes 1310720 | tf_op jit(solution)/shard_map/reduce_scatter | solution.py:375
  131.6 8.3 %collective-permute-start.2 = (bf16[15,2,256]{2,0,1:T(8,128)(2,1)S(1)}, bf16[15,2,256]{2,0,1:T(8,128)(2,1)S(1)}, u32[]{:S(2)}, u32[]{:S(2)}) collective-permute-start(bf16[15,2,256]{2,0,1:T(8,128)(2,1)S(1)} %get-tuple-element.100), channel_id=1, source_target_pairs={{0,4},{4,8},{8,12},{12,16},{16,20},{20,24},{24,28},{28,32},{32,36}... | collective-permute-start | bytes 46088 | tf_op jit(solution)/shard_map/ppermute | solution.py:214
  136.3 5.1 %collective-permute-start.3 = (bf16[15,2,256]{2,0,1:T(8,128)(2,1)S(1)}, bf16[15,2,256]{2,0,1:T(8,128)(2,1)S(1)}, u32[]{:S(2)}, u32[]{:S(2)}) collective-permute-start(bf16[15,2,256]{2,0,1:T(8,128)(2,1)S(1)} %get-tuple-element.101), channel_id=1, source_target_pairs={{4,0},{8,4},{12,8},{16,12},{20,16},{24,20},{28,24},{32,28},{36,32}... | collective-permute-start | bytes 46088 | tf_op jit(solution)/shard_map/ppermute | solution.py:217
  184.9 11.3 %copy-start.42 = (f32[1,1,256]{2,0,1:T(1,128)S(1)}, f32[1,1,256]{2,0,1:T(1,128)}, u32[]{:S(2)}) copy-start(f32[1,1,256]{2,0,1:T(1,128)} %get-tuple-element.128) | copy-start | bytes 3076
  185.0 11.3 %copy-start.43 = (f32[1,1,256]{2,0,1:T(1,128)S(1)}, f32[1,1,256]{2,0,1:T(1,128)}, u32[]{:S(2)}) copy-start(f32[1,1,256]{2,0,1:T(1,128)} %get-tuple-element.129) | copy-start | bytes 3076
  185.0 11.3 %copy-start.44 = (f32[1,1,256]{2,0,1:T(1,128)S(1)}, f32[1,1,256]{2,0,1:T(1,128)}, u32[]{:S(2)}) copy-start(f32[1,1,256]{2,0,1:T(1,128)} %get-tuple-element.130) | copy-start | bytes 3076
  185.0 11.3 %copy-start.45 = (f32[1,1,256]{2,0,1:T(1,128)S(1)}, f32[1,1,256]{2,0,1:T(1,128)}, u32[]{:S(2)}) copy-start(f32[1,1,256]{2,0,1:T(1,128)} %get-tuple-element.131) | copy-start | bytes 3076
  185.0 11.3 %copy-start.46 = (f32[1,1,256]{2,0,1:T(1,128)S(1)}, f32[1,1,256]{2,0,1:T(1,128)}, u32[]{:S(2)}) copy-start(f32[1,1,256]{2,0,1:T(1,128)} %get-tuple-element.132) | copy-start | bytes 3076
  185.0 11.3 %copy-start.47 = (f32[1,1,256]{2,0,1:T(1,128)S(1)}, f32[1,1,256]{2,0,1:T(1,128)}, u32[]{:S(2)}) copy-start(f32[1,1,256]{2,0,1:T(1,128)} %get-tuple-element.133) | copy-start | bytes 3076
  185.0 11.3 %copy-start.48 = (f32[1,1,256]{2,0,1:T(1,128)S(1)}, f32[1,1,256]{2,0,1:T(1,128)}, u32[]{:S(2)}) copy-start(f32[1,1,256]{2,0,1:T(1,128)} %get-tuple-element.134) | copy-start | bytes 3076
  185.0 11.3 %copy-start.49 = (f32[1,1,256]{2,0,1:T(1,128)S(1)}, f32[1,1,256]{2,0,1:T(1,128)}, u32[]{:S(2)}) copy-start(f32[1,1,256]{2,0,1:T(1,128)} %get-tuple-element.135) | copy-start | bytes 3076
  185.0 11.3 %copy-start.50 = (f32[1,1,256]{2,0,1:T(1,128)S(1)}, f32[1,1,256]{2,0,1:T(1,128)}, u32[]{:S(2)}) copy-start(f32[1,1,256]{2,0,1:T(1,128)} %get-tuple-element.145) | copy-start | bytes 3076
  185.0 11.3 %copy-start.52 = (f32[1,1,256]{2,0,1:T(1,128)S(1)}, f32[1,1,256]{2,0,1:T(1,128)}, u32[]{:S(2)}) copy-start(f32[1,1,256]{2,0,1:T(1,128)} %copy-done.51) | copy-start | bytes 3076
  185.1 11.3 %copy-start.54 = (f32[1,1,256]{2,0,1:T(1,128)S(1)}, f32[1,1,256]{2,0,1:T(1,128)}, u32[]{:S(2)}) copy-start(f32[1,1,256]{2,0,1:T(1,128)} %copy-done.53) | copy-start | bytes 3076
  185.1 11.3 %copy-start.56 = (f32[1,1,256]{2,0,1:T(1,128)S(1)}, f32[1,1,256]{2,0,1:T(1,128)}, u32[]{:S(2)}) copy-start(f32[1,1,256]{2,0,1:T(1,128)} %copy-done.55) | copy-start | bytes 3076
  185.1 11.3 %copy-start.58 = (f32[1,1,256]{2,0,1:T(1,128)S(1)}, f32[1,1,256]{2,0,1:T(1,128)}, u32[]{:S(2)}) copy-start(f32[1,1,256]{2,0,1:T(1,128)} %copy-done.57) | copy-start | bytes 3076
  185.1 11.3 %copy-start.60 = (f32[1,1,256]{2,0,1:T(1,128)S(1)}, f32[1,1,256]{2,0,1:T(1,128)}, u32[]{:S(2)}) copy-start(f32[1,1,256]{2,0,1:T(1,128)} %copy-done.59) | copy-start | bytes 3076
  185.1 11.3 %copy-start.62 = (f32[1,1,256]{2,0,1:T(1,128)S(1)}, f32[1,1,256]{2,0,1:T(1,128)}, u32[]{:S(2)}) copy-start(f32[1,1,256]{2,0,1:T(1,128)} %copy-done.61) | copy-start | bytes 3076
  186.6 6.6 %collective-permute-start.4 = (bf16[15,2,256]{2,0,1:T(8,128)(2,1)S(1)}, bf16[15,2,256]{2,0,1:T(8,128)(2,1)S(1)}, u32[]{:S(2)}, u32[]{:S(2)}) collective-permute-start(bf16[15,2,256]{2,0,1:T(8,128)(2,1)S(1)} %get-tuple-element.98), channel_id=1, source_target_pairs={{0,4},{4,8},{8,12},{12,16},{16,20},{20,24},{24,28},{28,32},{32,36}... | collective-permute-start | bytes 46088 | tf_op jit(solution)/shard_map/ppermute | solution.py:214
  191.0 5.1 %collective-permute-start.5 = (bf16[15,2,256]{2,0,1:T(8,128)(2,1)S(1)}, bf16[15,2,256]{2,0,1:T(8,128)(2,1)S(1)}, u32[]{:S(2)}, u32[]{:S(2)}) collective-permute-start(bf16[15,2,256]{2,0,1:T(8,128)(2,1)S(1)} %get-tuple-element.99), channel_id=1, source_target_pairs={{4,0},{8,4},{12,8},{16,12},{20,16},{24,20},{28,24},{32,28},{36,32}... | collective-permute-start | bytes 46088 | tf_op jit(solution)/shard_map/ppermute | solution.py:217
  200.2 27.1 %copy-start.90 = (f32[1,256]{1,0:T(1,128)S(1)}, f32[1,256]{1,0:T(1,128)}, u32[]{:S(2)}) copy-start(f32[1,256]{1,0:T(1,128)} %copy-done.89) | copy-start | bytes 3076
  200.2 27.1 %copy-start.127 = (f32[1,256]{1,0:T(1,128)S(1)}, f32[1,256]{1,0:T(1,128)}, u32[]{:S(2)}) copy-start(f32[1,256]{1,0:T(1,128)} %get-tuple-element.178) | copy-start | bytes 3076
  200.2 53.9 %copy-start.124 = (f32[1,256]{1,0:T(1,128)S(1)}, f32[1,256]{1,0:T(1,128)}, u32[]{:S(2)}) copy-start(f32[1,256]{1,0:T(1,128)} %copy-done.123) | copy-start | bytes 3076
  200.2 53.9 %copy-start.136 = (f32[1,256]{1,0:T(1,128)S(1)}, f32[1,256]{1,0:T(1,128)}, u32[]{:S(2)}) copy-start(f32[1,256]{1,0:T(1,128)} %get-tuple-element.180) | copy-start | bytes 3076
  201.7 52.4 %all-gather.11.cloned.1.call-start = ((), (), s32[]{:S(2)}) async-start(), calls=%async_computation.8 | async-start | bytes 1310720 | tf_op jit(solution)/shard_map/all_gather | solution.py:325
  227.2 28.9 %copy-start.134 = (f32[8]{0:T(128)S(1)}, f32[8]{0:T(128)}, u32[]{:S(2)}) copy-start(f32[8]{0:T(128)} %pad.11.clone) | copy-start | bytes 100
  227.2 155.8 %reduce-scatter.8.cloned.1.call-start = ((), (), s32[]{:S(2)}) async-start(), calls=%async_computation.9 | async-start | bytes 1310720 | tf_op jit(solution)/shard_map/reduce_scatter | solution.py:375
  276.8 8.4 %collective-permute-start.6 = (bf16[15,2,256]{2,0,1:T(8,128)(2,1)S(1)}, bf16[15,2,256]{2,0,1:T(8,128)(2,1)S(1)}, u32[]{:S(2)}, u32[]{:S(2)}) collective-permute-start(bf16[15,2,256]{2,0,1:T(8,128)(2,1)S(1)} %get-tuple-element.96), channel_id=1, source_target_pairs={{0,4},{4,8},{8,12},{12,16},{16,20},{20,24},{24,28},{28,32},{32,36}... | collective-permute-start | bytes 46088 | tf_op jit(solution)/shard_map/ppermute | solution.py:214
  280.3 5.2 %collective-permute-start.7 = (bf16[15,2,256]{2,0,1:T(8,128)(2,1)S(1)}, bf16[15,2,256]{2,0,1:T(8,128)(2,1)S(1)}, u32[]{:S(2)}, u32[]{:S(2)}) collective-permute-start(bf16[15,2,256]{2,0,1:T(8,128)(2,1)S(1)} %get-tuple-element.97), channel_id=1, source_target_pairs={{4,0},{8,4},{12,8},{16,12},{20,16},{24,20},{28,24},{32,28},{36,32}... | collective-permute-start | bytes 46088 | tf_op jit(solution)/shard_map/ppermute | solution.py:217
  292.7 44.3 %copy-start.91 = (f32[1,256]{1,0:T(1,128)S(1)}, f32[1,256]{1,0:T(1,128)}, u32[]{:S(2)}) copy-start(f32[1,256]{1,0:T(1,128)} %copy-done.89) | copy-start | bytes 3076
  341.8 41.3 %copy-start.22 = (f32[64,2]{0,1:T(2,128)S(1)}, f32[64,2]{0,1:T(2,128)}, u32[]{:S(2)}) copy-start(f32[64,2]{0,1:T(2,128)} %copy-done.21) | copy-start | bytes 1540
  341.8 42.5 %copy-start.7 = (bf16[64,2,1024]{2,0,1:T(8,128)(2,1)S(1)}, bf16[64,2,1024]{2,0,1:T(8,128)(2,1)}, u32[]{:S(2)}) copy-start(bf16[64,2,1024]{2,0,1:T(8,128)(2,1)} %reduce-scatter.6.cloned.1.call-done) | copy-start | bytes 786436
  (106 other events, 625.9 us)
Sparse Core Ops, SparseCore 0:
  11.6 29.3 all-gather.4
  77.3 21.9 reduce-scatter.3
  101.8 26.6 all-gather.6
  130.2 26.8 all-gather.8
  201.8 22.1 reduce-scatter.5
  227.4 26.6 all-gather.10
  292.9 24.0 reduce-scatter.7

commit v2 on v0

v2 whole, which is shorter than its diff:
```python
import functools

import jax
import jax.numpy as jnp
from jax import lax
from jax.experimental import pallas as pl
from jax.experimental.pallas import tpu as pltpu
from jax.sharding import PartitionSpec as P

EPSILON = 1e-05
MESH = pl.DeviceIdType.MESH
F32, BF16 = jnp.float32, jnp.bfloat16
TAPS, REACH = 31, 15
LANES = 128
STREAMS, SEG = 4, 16
ROWS = SEG * 8
MAIN = REACH * 8
WIDE = (SEG + 2 * REACH) * 8


def grid_of(ctx):
    return {64: (4, 8, 2), 8: (2, 2, 2)}[ctx]


def rows_of(slot, first=0, count=ROWS):
    return pl.ds(pl.multiple_of(slot * ROWS + first, 16), count)


def sigmoid(v):
    return 1.0 / (1.0 + jnp.exp(-v))


def fused(
    ctx,
    tp,
    frames,
    og,
    lengths,
    vw,
    gw,
    pw,
    taps,
    gain,
    shift,
    up,
    value_out,
    gate_out,
    project_out,
    tap_out,
    val,
    gath,
    ups,
    part,
    land,
    normed,
    lnscale,
    fv,
    fg,
    scaled,
    ds,
    act,
    glu,
    wide,
    lows,
    halo,
    first,
    second,
    tapsum,
    tap1,
    tap2,
    wt,
    in1,
    out2,
    in2,
    out3,
    in3,
    ssem,
    rsem,
):
    ny, nz, nc = grid_of(ctx)
    pos = lax.axis_index("ctx")
    x = lax.axis_index("tp")
    y, z, c = pos // (nz * nc), (pos // nc) % nz, pos % nc
    depth = gath.shape[2]
    columns = value_out.shape[2]

    def to_x(p):
        return {"tp": p}

    def to_yc(p):
        return {"ctx": ((p // nc) * nz + z) * nc + p % nc}

    def to_y(p):
        return {"ctx": (p * nz + z) * nc + c}

    def to_z(p):
        return {"ctx": (y * nz + p) * nc + c}

    def to_c(p):
        return {"ctx": (y * nz + z) * nc + p}

    yc = y * nc + c
    following = {"ctx": lax.rem(pos + 1, ctx)}
    previous = {"ctx": lax.rem(pos + ctx - 1, ctx)}

    barrier = pltpu.get_barrier_semaphore()
    peers = [to_x(lax.rem(x + s, tp)) for s in range(1, tp)]
    peers += [to_yc(lax.rem(yc + s, ny * nc)) for s in range(1, ny * nc)]
    peers += [to_z(lax.rem(z + s, nz)) for s in range(1, nz)]
    peers += [following, previous]
    for peer in peers:
        pl.semaphore_signal(barrier, inc=1, device_id=peer, device_id_type=MESH)
    pl.semaphore_wait(barrier, len(peers))

    taken = [0]

    def take(n):
        taken[0] += n
        return taken[0] - n

    def remote(src, dst, send, recv, target):
        return pltpu.make_async_remote_copy(
            src_ref=src,
            dst_ref=dst,
            send_sem=ssem.at[send],
            recv_sem=rsem.at[recv],
            device_id=target,
            device_id_type=MESH,
        )

    class Exchange:
        def __init__(self, count, me, target, src, dst, order=None):
            self.count, self.me, self.target, self.src, self.dst = count, me, target, src, dst
            self.base = take(count)
            self.order = order or list(range(1, count))

        def peer(self, step):
            return lax.rem(self.me + step, self.count)

        def send(self, step):
            p = self.peer(step)
            remote(
                self.src(p), self.dst(self.me), self.base + step, self.base + self.me, self.target(p)
            ).start()

        def start(self):
            for step in self.order:
                self.send(step)

        def landed(self, step):
            p = self.peer(step)
            remote(
                self.src(p), self.dst(p), self.base + step, self.base + p, self.target(p)
            ).wait_recv()

        def sent(self):
            for step in self.order:
                p = self.peer(step)
                remote(
                    self.src(p), self.dst(self.me), self.base + step, self.base + self.me, self.target(p)
                ).wait_send()

        def finish(self):
            for step in self.order:
                self.landed(step)
            self.sent()

    far_last = [1, 3, 2] if tp == 4 else list(range(1, tp))
    far_first = [2, 1, 3] if tp == 4 else list(range(1, tp))

    len0, len1 = lengths[0], lengths[1]
    start_frame = pos * (tp * STREAMS * SEG)
    t_in = lax.broadcasted_iota(jnp.int32, (SEG, 8, LANES), 0)
    sub = lax.broadcasted_iota(jnp.int32, (SEG, 8, LANES), 1)
    limit = jnp.where(sub % 2 == 0, len0, len1)
    for s in range(tp):
        frame = start_frame + s * (STREAMS * SEG) + (sub // 2) * SEG + t_in
        val[s] = jnp.where(frame < limit, 1.0, 0.0).astype(F32).reshape(ROWS, LANES)
    span = tp * STREAMS * SEG
    total = (len0 + len1).astype(F32)
    local_count = (
        jnp.clip(len0 - start_frame, 0, span) + jnp.clip(len1 - start_frame, 0, span)
    ).astype(F32)

    def halves(h):
        return slice(h * LANES, (h + 1) * LANES)

    def reduce_tile(u, rows, merge, meanwhile=None):
        first[u, yc] = jnp.zeros((8, LANES), F32)
        for i, row in enumerate(rows):
            first[u, yc, i : i + 1, :] = row
        one = Exchange(
            ny * nc, yc, to_yc, lambda p: first.at[u, yc], lambda p: first.at[u, p]
        )
        one.start()
        if meanwhile is not None:
            meanwhile()
        one.finish()
        second[u, z] = merge([first[u, i] for i in range(ny * nc)])
        two = Exchange(nz, z, to_z, lambda p: second.at[u, z], lambda p: second.at[u, p])
        two.start()
        two.finish()
        return merge([second[u, i] for i in range(nz)])

    def merge_sum(tiles):
        whole = tiles[0]
        for tile in tiles[1:]:
            whole = whole + tile
        return whole

    def merge_moments(tiles):
        whole = merge_sum(tiles)
        mean = whole[0:2] / jnp.maximum(whole[4:5], 1.0)
        square = whole[2:4]
        for tile in tiles:
            gap = tile[0:2] / jnp.maximum(tile[4:5], 1.0) - mean
            square = square + tile[4:5] * gap * gap
        return jnp.concatenate([whole[0:2], square, whole[4:8]], axis=0)

    def fold(v):
        return jnp.sum(v.reshape(SEG, 8, LANES), axis=0)

    tile_sub = lax.broadcasted_iota(jnp.int32, (REACH, 8, LANES), 1)

    def widen(e, s):
        for h in range(2):
            cur = wide[e, h, s, MAIN + 8 : MAIN + ROWS].reshape(REACH, 8, LANES)
            old = wide[e, h, s - 1, MAIN + 8 : MAIN + ROWS].reshape(REACH, 8, LANES)
            low = jnp.where(tile_sub < 2, pltpu.roll(old, 2, 1), pltpu.roll(cur, 2, 1))
            wide[e, h, s, 0:MAIN] = low.reshape(MAIN, LANES)
            cur = wide[e, h, s, MAIN : MAIN + ROWS - 8].reshape(REACH, 8, LANES)
            new = wide[e, h, s + 1, MAIN : MAIN + ROWS - 8].reshape(REACH, 8, LANES)
            high = jnp.where(tile_sub >= 6, pltpu.roll(new, 6, 1), pltpu.roll(cur, 6, 1))
            wide[e, h, s, MAIN + ROWS : WIDE] = high.reshape(MAIN, LANES)

    def convolve(e, layer, h, s, forward):
        result = None
        for j in range(TAPS):
            at = (j if forward else TAPS - 1 - j) * 8
            term = taps[layer, j : j + 1, halves(h)] * wide[e, h, s, at : at + ROWS]
            result = term if result is None else result + term
        return result

    class Halo:
        def __init__(self, u):
            self.u = u
            base = take(2)
            self.up = remote(
                glu.at[rows_of(tp - 1)], halo.at[u, 0], base, base, following
            )
            self.down = remote(glu.at[rows_of(0)], halo.at[u, 1], base + 1, base + 1, previous)

        def start(self):
            self.up.start()
            self.down.start()

        def finish(self, e):
            self.up.wait()
            self.down.wait()
            has_low = (pos > 0).astype(F32)
            has_high = (pos < ctx - 1).astype(F32)
            for h in range(2):
                wide[e, h, 0, MAIN : MAIN + ROWS] = halo[self.u, 0, :, halves(h)].astype(F32) * has_low
                wide[e, h, tp + 1, MAIN : MAIN + ROWS] = (
                    halo[self.u, 1, :, halves(h)].astype(F32) * has_high
                )

    class Scatter:
        def __init__(self, layer):
            self.layer = layer
            other = lax.rem(c + 1, nc)
            base = take(1)
            self.core = remote(
                wt.at[layer, :, :, :, other], in1.at[layer], base, base, to_c(other)
            )
            self.ys = Exchange(
                ny, y, to_y, lambda p: out2.at[layer, :, p], lambda p: in2.at[layer, p]
            )
            self.zs = Exchange(
                nz, z, to_z, lambda p: out3.at[layer, :, p], lambda p: in3.at[layer, p]
            )

        def start(self):
            self.core.start()

        def after_core(self):
            layer = self.layer
            self.core.wait()

            def add(i, carry):
                a, b = i // ny, i % ny
                out2[layer, a, b] = (
                    wt[layer, a, b, :, c].astype(F32) + in1[layer, a, b].astype(F32)
                ).astype(BF16)
                return carry

            lax.fori_loop(0, 3 * ny, add, 0)
            self.ys.start()

        def after_y(self):
            layer = self.layer
            self.ys.finish()

            def add(a, carry):
                whole = out2[layer, a, y].astype(F32)
                for s in range(1, ny):
                    whole = whole + in2[layer, lax.rem(y + s, ny), a].astype(F32)
                out3[layer, a] = whole.astype(BF16)
                return carry

            lax.fori_loop(0, 3, add, 0)
            self.zs.start()

        def after_z(self):
            layer = self.layer
            self.zs.finish()
            for a, out in enumerate((value_out, gate_out, project_out)):
                whole = out3[layer, a, z].astype(F32)
                for s in range(1, nz):
                    whole = whole + in3[layer, lax.rem(z + s, nz), a].astype(F32)
                out[layer] = whole

    def weight_term(left, right, put):
        def step(i, carry):
            cols = pl.ds(pl.multiple_of(i * (depth // ny), depth // ny), depth // ny)
            whole = lax.dot_general(
                left[:, cols], right[...], (((0,), (0,)), ((), ())), preferred_element_type=F32
            )
            put(i, whole.astype(BF16))
            return carry

        lax.fori_loop(0, ny, step, 0)

    class TapSum:
        def __init__(self, layer):
            self.layer = layer
            self.one = Exchange(
                ny * nc, yc, to_yc, lambda p: tap1.at[layer, yc], lambda p: tap1.at[layer, p]
            )
            self.two = Exchange(
                nz, z, to_z, lambda p: tap2.at[layer, z], lambda p: tap2.at[layer, p]
            )

        def start(self):
            tap1[self.layer, yc] = tapsum[...].astype(BF16)
            self.one.start()

        def middle(self):
            self.one.finish()
            whole = tap1[self.layer, 0].astype(F32)
            for i in range(1, ny * nc):
                whole = whole + tap1[self.layer, i].astype(F32)
            tap2[self.layer, z] = whole.astype(BF16)
            self.two.start()

        def finish(self):
            self.two.finish()
            whole = tap2[self.layer, 0].astype(F32)
            for i in range(1, nz):
                whole = whole + tap2[self.layer, i].astype(F32)
            for h in range(2):
                tap_out[self.layer, :, halves(h)] = whole[h, 0:TAPS]

    CHUNK = 32

    def normalize(layer, rows_at):
        def step(i, carry):
            at = pl.ds(pl.multiple_of(i * CHUNK, CHUNK), CHUNK)
            rows = rows_at(i * CHUNK, at)
            centered = rows - jnp.mean(rows, axis=1, keepdims=True)
            scale = lax.rsqrt(jnp.mean(centered * centered, axis=1, keepdims=True) + EPSILON)
            out = centered * scale
            normed[layer, at] = out
            lnscale[layer, at] = jnp.broadcast_to(scale, (CHUNK, LANES))
            gath[layer, rows_of(x, i * CHUNK, CHUNK)] = out.astype(BF16)
            return carry

        lax.fori_loop(0, ROWS // CHUNK, step, 0)

    def landed_sum(u, first_row):
        whole = part[rows_of(x, first_row, CHUNK)].astype(F32)
        for s in range(1, tp):
            whole = whole + land[u, rows_of(lax.rem(x + s, tp), first_row, CHUNK)].astype(F32)
        return whole

    def gather_x(buf, which):
        return Exchange(
            tp,
            x,
            to_x,
            lambda p: buf.at[which, rows_of(x)],
            lambda p: buf.at[which, rows_of(p)],
            far_last,
        )

    def scatter_x(u):
        return Exchange(
            tp,
            x,
            to_x,
            lambda p: part.at[rows_of(p)],
            lambda p: land.at[u, rows_of(p)],
            far_first,
        )

    def back_rows(layer, u, put):
        def step(i, carry):
            at = pl.ds(pl.multiple_of(i * CHUNK, CHUNK), CHUNK)
            grad = landed_sum(u, i * CHUNK)
            unit = normed[layer, at]
            cross = jnp.mean(grad * unit, axis=1, keepdims=True)
            scale = lnscale[layer, at][:, 0:1]
            put(i, at, scale * (grad - jnp.mean(grad, axis=1, keepdims=True) - unit * cross))
            return carry

        lax.fori_loop(0, ROWS // CHUNK, step, 0)

    def forward(layer, after=None):
        gather = gather_x(gath, layer)
        gather.start()
        if after is not None:
            after()

        def block(s):
            rows = gath[layer, rows_of(s)]
            value = jnp.dot(rows, vw[layer], preferred_element_type=F32)
            gate = sigmoid(jnp.dot(rows, gw[layer], preferred_element_type=F32))
            for h in range(2):
                v, g = value[:, halves(h)], gate[:, halves(h)]
                keep = g * val[s]
                fv[layer, h, s] = keep
                fg[layer, h, s] = v * (1.0 - g) * keep
                low = (v * keep).astype(BF16)
                glu[rows_of(s), halves(h)] = low
                wide[layer, h, s + 1, MAIN : MAIN + ROWS] = low.astype(F32)

        def order(k):
            return lax.rem(x + k + (k == 2).astype(jnp.int32) - (k == 3).astype(jnp.int32), tp)

        block(x)
        for step in far_last:
            gather.landed(step)
            block(gather.peer(step))
        gather.sent()
        edge = Halo(layer)
        edge.start()

        def conv(s, carry):
            widen(layer, s + 1)
            sums = []
            for h in range(2):
                mixed = convolve(layer, layer, h, s + 1, True)
                scaled[layer, h, s] = mixed
                sums.append(carry[h] + fold(mixed * val[s]))
            return tuple(sums)

        zero = jnp.zeros((8, LANES), F32)
        sums = lax.fori_loop(1, tp - 1, conv, (zero, zero))
        edge.finish(layer)
        sums = lax.fori_loop(0, 2, lambda i, carry: conv(i * (tp - 1), carry), sums)
        sums = [jnp.sum(v, axis=0, keepdims=True) for v in sums]
        means = [v / jnp.maximum(local_count, 1.0) for v in sums]

        def spread(s, carry):
            out = []
            for h in range(2):
                gap = (scaled[layer, h, s] - means[h]) * val[s]
                out.append(carry[h] + fold(gap * gap))
            return tuple(out)

        squares = lax.fori_loop(0, tp, spread, (zero, zero))
        squares = [jnp.sum(v, axis=0, keepdims=True) for v in squares]
        count = jnp.zeros((1, LANES), F32) + local_count
        whole = reduce_tile(layer, sums + squares + [count], merge_moments)
        mean = [whole[h : h + 1] / total for h in range(2)]
        scale = [lax.rsqrt(whole[2 + h : 3 + h] / total + EPSILON) for h in range(2)]

        def activate(s):
            for h in range(2):
                unit = (scaled[layer, h, s] - mean[h]) * scale[h]
                shifted = gain[layer : layer + 1, halves(h)] * unit + shift[layer : layer + 1, halves(h)]
                sig = sigmoid(shifted)
                keep = sig * val[s]
                scaled[layer, h, s] = unit
                ds[layer, h, s] = keep * (1.0 + shifted * (1.0 - sig))
                act[layer, rows_of(s), halves(h)] = (shifted * keep).astype(BF16)

        return activate, scale

    def backward(layer, u, up_block, chan_scale, activate, between, after_send):
        zero = jnp.zeros((8, LANES), F32)

        def one_block(s, carry):
            if activate is not None:
                activate(s)
            grad = lax.dot_general(
                ups[layer, rows_of(s)], pw[layer], (((1,), (1,)), ((), ())), preferred_element_type=F32
            )
            sums = list(carry)
            for h in range(2):
                g = grad[:, halves(h)] * ds[layer, h, s]
                ds[layer, h, s] = g
                sums[h] = sums[h] + fold(g)
                sums[2 + h] = sums[2 + h] + fold(g * scaled[layer, h, s])
            return tuple(sums)

        sums = up_block(one_block, (zero,) * 4)
        sums = [jnp.sum(v, axis=0, keepdims=True) for v in sums]

        def project():
            def put(i, block):
                wt[layer, 2, i] = block.reshape(wt.shape[3:])

            weight_term(ups.at[layer], act.at[layer], put)

        whole = reduce_tile(2 + layer, sums, merge_sum, project)

        def mix(s, carry):
            for h in range(2):
                factor = gain[layer : layer + 1, halves(h)] * chan_scale[h]
                a, b = whole[h : h + 1] / total, whole[2 + h : 3 + h] / total
                grad = factor * (ds[layer, h, s] - a - scaled[layer, h, s] * b) * val[s]
                wide[2, h, s + 1, MAIN : MAIN + ROWS] = grad
                glu[rows_of(s), halves(h)] = grad.astype(BF16)
            return carry

        lax.fori_loop(0, tp, mix, 0)
        edge = Halo(2 + layer)
        edge.start()

        def tap(j, carry):
            at = pl.ds(pl.multiple_of(j * 8, 8), ROWS)
            for h in range(2):
                whole = None
                for s in range(1, tp + 1):
                    term = fold(wide[layer, h, s, at] * wide[2, h, s, MAIN : MAIN + ROWS])
                    whole = term if whole is None else whole + term
                tapsum[h, pl.ds(j, 1), :] = jnp.sum(whole, axis=0, keepdims=True)
            return carry

        lax.fori_loop(0, TAPS, tap, 0)
        tap_total = TapSum(layer)
        edge.finish(2)
        tap_total.start()
        between()

        send = scatter_x(u)

        def block(s):
            widen(2, s + 1)
            for h in range(2):
                grad = convolve(2, layer, h, s + 1, False)
                lows[rows_of(s), halves(h)] = (grad * fv[layer, h, s]).astype(BF16)
                lows[rows_of(s), slice(columns + h * LANES, columns + (h + 1) * LANES)] = (
                    grad * fg[layer, h, s]
                ).astype(BF16)
            whole = lax.dot_general(
                lows[rows_of(s), 0:columns],
                vw[layer],
                (((1,), (1,)), ((), ())),
                preferred_element_type=F32,
            ) + lax.dot_general(
                lows[rows_of(s), columns : 2 * columns],
                gw[layer],
                (((1,), (1,)), ((), ())),
                preferred_element_type=F32,
            )
            part[rows_of(s)] = whole.astype(BF16)

        for step in far_first:
            block(send.peer(step))
            send.send(step)
        block(x)

        def put(i, block):
            wt[layer, 0, i] = block[:, 0:columns].reshape(wt.shape[3:])
            wt[layer, 1, i] = block[:, columns:].reshape(wt.shape[3:])

        weight_term(gath.at[layer], lows, put)
        scatter = Scatter(layer)
        scatter.start()
        after_send(scatter, tap_total)
        send.finish()
        return scatter, tap_total

    tapsum[...] = jnp.zeros(tapsum.shape, F32)
    normalize(0, lambda first_row, at: frames[at].astype(F32))
    gather_up = gather_x(ups, 1)

    def send_up():
        ups[1, rows_of(x)] = og[...]
        gather_up.start()

    activate, scale0 = forward(0, send_up)
    branch = scatter_x(0)

    def project_block(s):
        activate(s)
        part[rows_of(s)] = jnp.dot(
            act[0, rows_of(s)], pw[0], preferred_element_type=F32
        ).astype(BF16)

    for step in far_first:
        project_block(branch.peer(step))
        branch.send(step)
    project_block(x)
    branch.finish()

    def hidden(first_row, at):
        return (frames[at].astype(F32) + landed_sum(0, first_row)).astype(BF16).astype(F32)

    normalize(1, hidden)
    activate, scale1 = forward(1)
    gather_up.finish()

    def all_blocks(block, carry):
        return lax.fori_loop(0, tp, block, carry)

    scatter1, taps1 = backward(
        1, 1, all_blocks, scale1, activate, lambda: None, lambda scatter, tap_total: tap_total.middle()
    )

    def next_up(i, at, grad):
        whole = og[at].astype(F32) + grad
        up[at] = whole
        ups[0, rows_of(x, i * CHUNK, CHUNK)] = whole.astype(BF16)

    back_rows(1, 1, next_up)
    gather0 = gather_x(ups, 0)
    gather0.start()
    scatter1.after_core()
    taps1.finish()

    def in_turn(block, carry):
        carry = block(x, carry)
        for step in far_last:
            gather0.landed(step)
            carry = block(gather0.peer(step), carry)
        gather0.sent()
        return carry

    def finish_first(scatter, tap_total):
        tap_total.middle()
        scatter.after_core()
        scatter1.after_z()

    scatter0, taps0 = backward(0, 2, in_turn, scale0, None, scatter1.after_y, finish_first)

    def last_up(i, at, grad):
        up[at] = up[at] + grad

    back_rows(0, 2, last_up)
    scatter0.after_y()
    taps0.finish()
    scatter0.after_z()


def scratch(ctx, tp, layers, depth, columns):
    ny, nz, nc = grid_of(ctx)
    rows = tp * ROWS
    piece = depth // ctx
    return [
        pltpu.VMEM((tp, ROWS, LANES), F32),
        pltpu.VMEM((layers, rows, depth), BF16),
        pltpu.VMEM((layers, rows, depth), BF16),
        pltpu.VMEM((rows, depth), BF16),
        pltpu.VMEM((3, rows, depth), BF16),
        pltpu.VMEM((layers, ROWS, depth), F32),
        pltpu.VMEM((layers, ROWS, LANES), F32),
        pltpu.VMEM((layers, 2, tp, ROWS, LANES), F32),
        pltpu.VMEM((layers, 2, tp, ROWS, LANES), F32),
        pltpu.VMEM((layers, 2, tp, ROWS, LANES), F32),
        pltpu.VMEM((layers, 2, tp, ROWS, LANES), F32),
        pltpu.VMEM((layers, rows, columns), BF16),
        pltpu.VMEM((rows, columns), BF16),
        pltpu.VMEM((3, 2, tp + 2, WIDE, LANES), F32),
        pltpu.VMEM((rows, 2 * columns), BF16),
        pltpu.VMEM((4, 2, ROWS, columns), BF16),
        pltpu.VMEM((4, ny * nc, 8, LANES), F32),
        pltpu.VMEM((4, nz, 8, LANES), F32),
        pltpu.VMEM((2, TAPS + 1, LANES), F32),
        pltpu.VMEM((layers, ny * nc, 2, TAPS + 1, LANES), BF16),
        pltpu.VMEM((layers, nz, 2, TAPS + 1, LANES), BF16),
        pltpu.VMEM((layers, 3, ny, nz, nc, piece, columns), BF16),
        pltpu.VMEM((layers, 3, ny, nz, piece, columns), BF16),
        pltpu.VMEM((layers, 3, ny, nz, piece, columns), BF16),
        pltpu.VMEM((layers, ny, 3, nz, piece, columns), BF16),
        pltpu.VMEM((layers, 3, nz, piece, columns), BF16),
        pltpu.VMEM((layers, nz, 3, piece, columns), BF16),
        pltpu.SemaphoreType.DMA((192,)),
        pltpu.SemaphoreType.DMA((192,)),
    ]


def shuffled(rows):
    frames, recs, depth = rows.shape
    return (
        rows.reshape(STREAMS, SEG, recs, depth).transpose(1, 0, 2, 3).reshape(frames * recs, depth)
    )


def restored(rows, recs):
    count, depth = rows.shape
    return (
        rows.reshape(SEG, STREAMS, recs, depth).transpose(1, 0, 2, 3).reshape(count // recs, recs, depth)
    )


def on_device(
    frames,
    lengths,
    value_weight,
    gate_weight,
    tap_weights,
    norm_gain,
    norm_shift,
    project_weight,
    output_grad,
):
    ctx, tp = lax.axis_size("ctx"), lax.axis_size("tp")
    layers, depth, columns = value_weight.shape
    piece = depth // ctx
    vmem = pl.BlockSpec(memory_space=pltpu.VMEM)
    smem = pl.BlockSpec(memory_space=pltpu.SMEM)
    up, value, gate, project, tap = pl.pallas_call(
        functools.partial(fused, ctx, tp),
        out_shape=(
            jax.ShapeDtypeStruct((ROWS, depth), F32),
            jax.ShapeDtypeStruct((layers, piece, columns), F32),
            jax.ShapeDtypeStruct((layers, piece, columns), F32),
            jax.ShapeDtypeStruct((layers, piece, columns), F32),
            jax.ShapeDtypeStruct((layers, TAPS, columns), F32),
        ),
        in_specs=[vmem, vmem, smem, vmem, vmem, vmem, vmem, vmem, vmem],
        out_specs=(vmem,) * 5,
        scratch_shapes=scratch(ctx, tp, layers, depth, columns),
        compiler_params=pltpu.CompilerParams(
            collective_id=0, has_side_effects=True, vmem_limit_bytes=60 * 1024 * 1024
        ),
    )(
        shuffled(frames),
        shuffled(output_grad),
        lengths,
        value_weight,
        gate_weight,
        project_weight,
        tap_weights,
        norm_gain,
        norm_shift,
    )
    return restored(up, frames.shape[1]), value, gate, jnp.swapaxes(project, 1, 2), tap


def solution(mesh):
    in_specs = (
        P(("ctx", "tp"), None, None),
        P(),
        P(None, None, "tp"),
        P(None, None, "tp"),
        P(None, None, "tp"),
        P(None, "tp"),
        P(None, "tp"),
        P(None, "tp", None),
        P(("ctx", "tp"), None, None),
    )
    out_specs = (
        P(("ctx", "tp"), None, None),
        P(None, "ctx", "tp"),
        P(None, "ctx", "tp"),
        P(None, "tp", "ctx"),
        P(None, None, "tp"),
    )
    return jax.shard_map(
        on_device, mesh=mesh, in_specs=in_specs, out_specs=out_specs, check_vma=False
    )
```

time: 1710 us -> 173 us (0.10)
  blocking collectives: 991 us -> 0 us
  waiting for transfers between devices: 584 us -> 0 us
  Pallas kernels: 0 us -> 162 us
  other arithmetic: 40.7 us -> 0 us
  matrix products: 33.6 us -> 0 us
  starting transfers between devices: 25.6 us -> 0 us
    psum x7 -> x0, blocking collectives: 991 us -> none  [the longest x2 254 us: on_device(): lax.psum(jnp.sum(((mixed - chan_mean) * valid) ** 2, axis=(0, 1)), 'ctx')]
    reduce_scatter x9 -> x0, waiting for transfers between devices: 504 us -> none  [the longest x2 282 us: on_device(): lax.psum_scatter(value_term, 'ctx', scatter_dimension=0, tiled=True)]
    pallas_call x0 -> x1, Pallas kernels: none -> 162 us  [on_device(): pl.pallas_call(functools.partial(fused, ctx, tp), out_shape=(jax.ShapeDty...]
    all_gather x4 -> x0, waiting for transfers between devices: 72.9 us -> none  [the longest x2 49.1 us: on_device(): forward_gathered = lax.all_gather(normed_low, 'tp', axis=0, tiled=True)]
    dot_general x17 -> x0, matrix products: 33.6 us -> none  [the longest x2 6.02 us: on_device(): jnp.einsum('tbc,tbd->cd', backward_activated, upstream_all, preferred_ele...]
    ppermute x8 -> x0, starting transfers between devices: 24.8 us -> none  [the longest x4 13.2 us: padded(): lax.ppermute(lax.slice_in_dim(block, block.shape[dim] - width, None, axis...]
    reduce_sum x15 -> x0, other arithmetic: 22.5 us -> none  [the longest x4 8.65 us: on_device(): jnp.sum(widened[offset:offset + frame_count] * mixed_grad, axis=(0, 1))]
  transfers between devices with their start and end apart: 21 -> 0, of which waited for: 14 -> 0; matrix products, arithmetic and copies ran while one was open for 3% -> 0% of each run, Pallas kernels for 0% -> 0%
where the time goes in v2:
time: 173 us
  Pallas kernels  162 us (94%)
  local copies, waits for them, and re-layouts  9.72 us (6%)
    pallas_call x1, Pallas kernels, on_device(): pl.pallas_call(functools.partial(fused, ctx, tp), out_shape=(jax.ShapeDty...  162 us
    unnamed x15, local copies, waits for them, and re-layouts  4.52 us

profile of v2, /device:TPU:1, one launch (start us, length us, event | category | flops | bytes accessed | tf_op | source)
XLA Modules:
  0.0 172.9 jit_solution(3794001650174875148)
XLA Ops:
  0.6 1.5 copy.16.taps
  2.1 1.2 copy.22
  3.3 0.0 copy-start
  3.3 0.8 reshape.29.frames
  4.1 0.1 copy-done
  4.2 0.2 copy.21
  4.5 0.8 reshape.31.og
  5.3 162.5 %shard_map.128 = (f32[128,1024]{1,0:T(8,128)}, f32[2,16,256]{2,1,0:T(8,128)}, f32[2,16,256]{2,1,0:T(8,128)}, f32[2,16,256]{2,1,0:T(8,128)}, f32[2,31,256]{2,1,0:T(8,128)}) custom-call(bf16[128,1024]{1,0:T(8,128)(2,1)} %reshape.29.frames, bf16[128,1024]{1,0:T(8,128)(2,1)} %reshape.31.og, s32[2]{0:T(128)} %lengths.1, bf16[2,1024,256]{2,1,0:T(8,128)(2,1)} %vw.1, ...), custom_call_target="tpu_custom_call" | custom-call | tf_op jit(solution)/shard_map/pallas_call | solution.py:725
  167.7 1.3 reshape.32
  169.1 0.0 copy-start.1
  169.1 0.8 copy.17
  169.9 0.0 copy-done.1
  169.9 0.0 copy-start.4
  170.0 0.7 copy.18
  170.6 0.1 copy-done.4
  170.7 0.0 copy-start.3
  170.7 0.6 copy.26
  171.3 0.2 copy-done.3
  171.5 0.0 copy-start.2
  171.5 0.6 copy.27
  172.1 0.2 copy-done.2
  172.3 0.6 copy.28
Async XLA Ops:
  3.3 1.0 copy-start
  169.1 0.9 copy-start.1
  169.9 0.8 copy-start.4
  170.7 0.8 copy-start.3
  171.5 0.8 copy-start.2

commit v3 on v2

--- a/solution.py
+++ b/solution.py
@@ -11,6 +11,7 @@
 MESH = pl.DeviceIdType.MESH
 F32, BF16 = jnp.float32, jnp.bfloat16
 TAPS, REACH = 31, 15
+CHUNK = 32
 LANES = 128
 STREAMS, SEG = 4, 16
 ROWS = SEG * 8
@@ -36,21 +37,27 @@
     frames,
     og,
     lengths,
-    vw,
-    gw,
-    pw,
+    vw_in,
+    gw_in,
+    pw_in,
     taps,
     gain,
     shift,
-    up,
+    up_out,
     value_out,
     gate_out,
     project_out,
     tap_out,
+    vw,
+    gw,
+    pw,
+    hid,
+    up,
     val,
     gath,
     ups,
     part,
+    farland,
     land,
     normed,
     lnscale,
@@ -74,6 +81,7 @@
     in2,
     out3,
     in3,
+    lsem,
     ssem,
     rsem,
 ):
@@ -110,7 +118,12 @@
     peers += [following, previous]
     for peer in peers:
         pl.semaphore_signal(barrier, inc=1, device_id=peer, device_id_type=MESH)
-    pl.semaphore_wait(barrier, len(peers))
+    loads = [
+        pltpu.make_async_copy(src, dst, lsem.at[i])
+        for i, (src, dst) in enumerate(((vw_in, vw), (gw_in, gw), (pw_in, pw)))
+    ]
+    for load in loads:
+        load.start()
 
     taken = [0]
 
@@ -129,10 +142,10 @@
         )
 
     class Exchange:
-        def __init__(self, count, me, target, src, dst, order=None):
+        def __init__(self, count, me, target, src, dst):
             self.count, self.me, self.target, self.src, self.dst = count, me, target, src, dst
             self.base = take(count)
-            self.order = order or list(range(1, count))
+            self.order = list(range(1, count))
 
         def peer(self, step):
             return lax.rem(self.me + step, self.count)
@@ -165,8 +178,121 @@
                 self.landed(step)
             self.sent()
 
-    far_last = [1, 3, 2] if tp == 4 else list(range(1, tp))
-    far_first = [2, 1, 3] if tp == 4 else list(range(1, tp))
+    right, left, far = lax.rem(x + 1, tp), lax.rem(x + 3, tp), lax.rem(x + 2, tp)
+
+    class GatherX:
+        def __init__(self, buf, which):
+            self.rows = lambda d, i: buf.at[which, rows_of(d, i * CHUNK, CHUNK)]
+            self.base = take(12)
+
+        def copy(self, owner, i, sem, target):
+            ref = self.rows(owner, i)
+            return remote(ref, ref, self.base + sem, self.base + sem, to_x(target))
+
+        def push(self, i):
+            self.copy(x, i, i, right).start()
+            self.copy(x, i, 4 + i, left).start()
+
+        def onward(self, i):
+            if i < 2:
+                self.copy(left, i, i, right).wait_recv()
+                self.copy(left, i, 8 + i, right).start()
+            else:
+                self.copy(right, i, 4 + i, left).wait_recv()
+                self.copy(right, i, 8 + i, left).start()
+
+        def wait_left(self):
+            for i in (2, 3):
+                self.copy(left, i, i, right).wait_recv()
+
+        def wait_right(self):
+            for i in (0, 1):
+                self.copy(right, i, 4 + i, left).wait_recv()
+
+        def wait_far(self):
+            for i in (0, 2, 1, 3):
+                self.copy(far, i, 8 + i, right).wait_recv()
+
+        def sent(self):
+            for i in range(4):
+                self.copy(x, i, i, right).wait_send()
+                self.copy(x, i, 4 + i, left).wait_send()
+                if i < 2:
+                    self.copy(left, i, 8 + i, right).wait_send()
+                else:
+                    self.copy(right, i, 8 + i, left).wait_send()
+
+    class ScatterX:
+        def __init__(self, u):
+            self.u = u
+            self.base = take(12)
+
+        def far_copy(self, i):
+            return remote(
+                part.at[rows_of(far, i * CHUNK, CHUNK)],
+                farland.at[self.u, pl.ds(i * CHUNK, CHUNK)],
+                self.base + i,
+                self.base + i,
+                to_x(right if i < 2 else left),
+            )
+
+        def near_copy(self, way, i):
+            sem = self.base + 4 + 4 * way + i
+            return remote(
+                part.at[rows_of(left if way else right, i * CHUNK, CHUNK)],
+                land.at[self.u, way, pl.ds(i * CHUNK, CHUNK)],
+                sem,
+                sem,
+                to_x(left if way else right),
+            )
+
+        def send_far(self):
+            for i in (0, 2, 1, 3):
+                self.far_copy(i).start()
+
+        def send_early(self):
+            self.near_copy(0, 2).start()
+            self.near_copy(1, 0).start()
+
+        def send_late(self):
+            self.near_copy(0, 3).start()
+            self.near_copy(1, 1).start()
+
+        def combine(self, i):
+            self.far_copy(i).wait_recv()
+            way = 0 if i < 2 else 1
+            at = rows_of(left if way else right, i * CHUNK, CHUNK)
+            part[at] = (
+                part[at].astype(F32) + farland[self.u, i * CHUNK : (i + 1) * CHUNK].astype(F32)
+            ).astype(BF16)
+            self.near_copy(way, i).start()
+
+        def combine_first(self):
+            self.combine(0)
+            self.combine(2)
+
+        def combine_last(self):
+            self.send_late()
+            self.combine(1)
+            self.combine(3)
+
+        def landed(self, i):
+            self.near_copy(0, i).wait_recv()
+            self.near_copy(1, i).wait_recv()
+
+        def sent(self):
+            for i in range(4):
+                self.far_copy(i).wait_send()
+                self.near_copy(0, i).wait_send()
+                self.near_copy(1, i).wait_send()
+
+        def rows(self, first_row):
+            at = pl.ds(pl.multiple_of(first_row, CHUNK), CHUNK)
+            return (
+                part[rows_of(x, first_row, CHUNK)].astype(F32)
+                + land[self.u, 0, at].astype(F32)
+                + land[self.u, 1, at].astype(F32)
+            )
 
     len0, len1 = lengths[0], lengths[1]
     start_frame = pos * (tp * STREAMS * SEG)
@@ -185,7 +311,7 @@
     def halves(h):
         return slice(h * LANES, (h + 1) * LANES)
 
-    def reduce_tile(u, rows, merge, meanwhile=None):
+    def reduce_tile(u, rows, merge, meanwhile=None, later=None):
         first[u, yc] = jnp.zeros((8, LANES), F32)
         for i, row in enumerate(rows):
             first[u, yc, i : i + 1, :] = row
@@ -199,6 +325,8 @@
         second[u, z] = merge([first[u, i] for i in range(ny * nc)])
         two = Exchange(nz, z, to_z, lambda p: second.at[u, z], lambda p: second.at[u, p])
         two.start()
+        if later is not None:
+            later()
         two.finish()
         return merge([second[u, i] for i in range(nz)])
 
@@ -237,7 +365,7 @@
         result = None
         for j in range(TAPS):
             at = (j if forward else TAPS - 1 - j) * 8
-            term = taps[layer, j : j + 1, halves(h)] * wide[e, h, s, at : at + ROWS]
+            term = taps[j, layer : layer + 1, halves(h)] * wide[e, h, s, at : at + ROWS]
             result = term if result is None else result + term
         return result
 
@@ -266,18 +394,19 @@
                 )
 
     class Scatter:
-        def __init__(self, layer):
-            self.layer = layer
+        def __init__(self, layer, low, high):
+            self.layer, self.low, self.high = layer, low, high
             other = lax.rem(c + 1, nc)
             base = take(1)
+            mats = slice(low, high)
             self.core = remote(
-                wt.at[layer, :, :, :, other], in1.at[layer], base, base, to_c(other)
+                wt.at[layer, mats, :, :, other], in1.at[layer, mats], base, base, to_c(other)
             )
             self.ys = Exchange(
-                ny, y, to_y, lambda p: out2.at[layer, :, p], lambda p: in2.at[layer, p]
+                ny, y, to_y, lambda p: out2.at[layer, mats, p], lambda p: in2.at[layer, p, mats]
             )
             self.zs = Exchange(
-                nz, z, to_z, lambda p: out3.at[layer, :, p], lambda p: in3.at[layer, p]
+                nz, z, to_z, lambda p: out3.at[layer, mats, p], lambda p: in3.at[layer, p, mats]
             )
 
         def start(self):
@@ -294,7 +423,7 @@
                 ).astype(BF16)
                 return carry
 
-            lax.fori_loop(0, 3 * ny, add, 0)
+            lax.fori_loop(self.low * ny, self.high * ny, add, 0)
             self.ys.start()
 
         def after_y(self):
@@ -308,13 +437,14 @@
                 out3[layer, a] = whole.astype(BF16)
                 return carry
 
-            lax.fori_loop(0, 3, add, 0)
+            lax.fori_loop(self.low, self.high, add, 0)
             self.zs.start()
 
         def after_z(self):
             layer = self.layer
             self.zs.finish()
-            for a, out in enumerate((value_out, gate_out, project_out)):
+            outs = (value_out, gate_out, project_out)
+            for a, out in list(enumerate(outs))[self.low : self.high]:
                 whole = out3[layer, a, z].astype(F32)
                 for s in range(1, nz):
                     whole = whole + in3[layer, lax.rem(z + s, nz), a].astype(F32)
@@ -359,68 +489,44 @@
             for i in range(1, nz):
                 whole = whole + tap2[self.layer, i].astype(F32)
             for h in range(2):
-                tap_out[self.layer, :, halves(h)] = whole[h, 0:TAPS]
-
-    CHUNK = 32
-
-    def normalize(layer, rows_at):
-        def step(i, carry):
-            at = pl.ds(pl.multiple_of(i * CHUNK, CHUNK), CHUNK)
-            rows = rows_at(i * CHUNK, at)
-            centered = rows - jnp.mean(rows, axis=1, keepdims=True)
-            scale = lax.rsqrt(jnp.mean(centered * centered, axis=1, keepdims=True) + EPSILON)
-            out = centered * scale
-            normed[layer, at] = out
-            lnscale[layer, at] = jnp.broadcast_to(scale, (CHUNK, LANES))
-            gath[layer, rows_of(x, i * CHUNK, CHUNK)] = out.astype(BF16)
+                tap_out[:, self.layer, halves(h)] = whole[h, 0:TAPS]
+
+    def pair(group, step):
+        lax.fori_loop(0, 2, lambda k, carry: step((2 * k + group) * CHUNK) or carry, 0)
+
+    def tiles(first_row):
+        return pl.ds(first_row // 8, CHUNK // 8)
+
+    def rows_in(ref, first_row):
+        return ref[tiles(first_row)].reshape(CHUNK, depth)
+
+    def fill(src, dst):
+        def step(t, carry):
+            for q in range(STREAMS):
+                dst[t, 2 * q : 2 * q + 2, :] = src[q, t].astype(F32)
             return carry
 
-        lax.fori_loop(0, ROWS // CHUNK, step, 0)
-
-    def landed_sum(u, first_row):
-        whole = part[rows_of(x, first_row, CHUNK)].astype(F32)
-        for s in range(1, tp):
-            whole = whole + land[u, rows_of(lax.rem(x + s, tp), first_row, CHUNK)].astype(F32)
-        return whole
-
-    def gather_x(buf, which):
-        return Exchange(
-            tp,
-            x,
-            to_x,
-            lambda p: buf.at[which, rows_of(x)],
-            lambda p: buf.at[which, rows_of(p)],
-            far_last,
-        )
-
-    def scatter_x(u):
-        return Exchange(
-            tp,
-            x,
-            to_x,
-            lambda p: part.at[rows_of(p)],
-            lambda p: land.at[u, rows_of(p)],
-            far_first,
-        )
-
-    def back_rows(layer, u, put):
-        def step(i, carry):
-            at = pl.ds(pl.multiple_of(i * CHUNK, CHUNK), CHUNK)
-            grad = landed_sum(u, i * CHUNK)
-            unit = normed[layer, at]
-            cross = jnp.mean(grad * unit, axis=1, keepdims=True)
-            scale = lnscale[layer, at][:, 0:1]
-            put(i, at, scale * (grad - jnp.mean(grad, axis=1, keepdims=True) - unit * cross))
-            return carry
-
-        lax.fori_loop(0, ROWS // CHUNK, step, 0)
-
-    def forward(layer, after=None):
-        gather = gather_x(gath, layer)
-        gather.start()
-        if after is not None:
-            after()
-
+        lax.fori_loop(0, SEG, step, 0)
+
+    def normalize(layer, rows_at, first_row):
+        at = pl.ds(pl.multiple_of(first_row, CHUNK), CHUNK)
+        rows = rows_at(first_row)
+        centered = rows - jnp.mean(rows, axis=1, keepdims=True)
+        scale = lax.rsqrt(jnp.mean(centered * centered, axis=1, keepdims=True) + EPSILON)
+        out = centered * scale
+        normed[layer, at] = out
+        lnscale[layer, at] = jnp.broadcast_to(scale, (CHUNK, LANES))
+        gath[layer, rows_of(x, first_row, CHUNK)] = out.astype(BF16)
+
+    def back_rows(layer, summed, first_row):
+        at = pl.ds(pl.multiple_of(first_row, CHUNK), CHUNK)
+        grad = summed.rows(first_row)
+        unit = normed[layer, at]
+        cross = jnp.mean(grad * unit, axis=1, keepdims=True)
+        scale = lnscale[layer, at][:, 0:1]
+        return scale * (grad - jnp.mean(grad, axis=1, keepdims=True) - unit * cross)
+
+    def forward(layer, gather, after, later):
         def block(s):
             rows = gath[layer, rows_of(s)]
             value = jnp.dot(rows, vw[layer], preferred_element_type=F32)
@@ -434,14 +540,18 @@
                 glu[rows_of(s), halves(h)] = low
                 wide[layer, h, s + 1, MAIN : MAIN + ROWS] = low.astype(F32)
 
-        def order(k):
-            return lax.rem(x + k + (k == 2).astype(jnp.int32) - (k == 3).astype(jnp.int32), tp)
-
+        gather.onward(0)
+        gather.onward(2)
         block(x)
-        for step in far_last:
-            gather.landed(step)
-            block(gather.peer(step))
-        gather.sent()
+        gather.onward(1)
+        gather.onward(3)
+        after()
+        gather.wait_left()
+        block(left)
+        gather.wait_right()
+        block(right)
+        gather.wait_far()
+        block(far)
         edge = Halo(layer)
         edge.start()
 
@@ -471,7 +581,7 @@
         squares = lax.fori_loop(0, tp, spread, (zero, zero))
         squares = [jnp.sum(v, axis=0, keepdims=True) for v in squares]
         count = jnp.zeros((1, LANES), F32) + local_count
-        whole = reduce_tile(layer, sums + squares + [count], merge_moments)
+        whole = reduce_tile(layer, sums + squares + [count], merge_moments, gather.sent, later)
         mean = [whole[h : h + 1] / total for h in range(2)]
         scale = [lax.rsqrt(whole[2 + h : 3 + h] / total + EPSILON) for h in range(2)]
 
@@ -487,7 +597,7 @@
 
         return activate, scale
 
-    def backward(layer, u, up_block, chan_scale, activate, between, after_send):
+    def backward(layer, u, up_block, chan_scale, activate, between, after_send, weights_first):
         zero = jnp.zeros((8, LANES), F32)
 
         def one_block(s, carry):
@@ -507,13 +617,19 @@
         sums = up_block(one_block, (zero,) * 4)
         sums = [jnp.sum(v, axis=0, keepdims=True) for v in sums]
 
+        scatters = [Scatter(layer, 2, 3), Scatter(layer, 0, 2)] if weights_first else [Scatter(layer, 0, 3)]
+
         def project():
             def put(i, block):
                 wt[layer, 2, i] = block.reshape(wt.shape[3:])
 
             weight_term(ups.at[layer], act.at[layer], put)
+            if weights_first:
+                scatters[0].start()
 
         whole = reduce_tile(2 + layer, sums, merge_sum, project)
+        if weights_first:
+            scatters[0].after_core()
 
         def mix(s, carry):
             for h in range(2):
@@ -543,10 +659,12 @@
         edge.finish(2)
         tap_total.start()
         between()
-
-        send = scatter_x(u)
-
-        def block(s):
+        if weights_first:
+            scatters[0].after_y()
+
+        send = ScatterX(u)
+
+        def lows_block(s):
             widen(2, s + 1)
             for h in range(2):
                 grad = convolve(2, layer, h, s + 1, False)
@@ -554,6 +672,8 @@
                 lows[rows_of(s), slice(columns + h * LANES, columns + (h + 1) * LANES)] = (
                     grad * fg[layer, h, s]
                 ).astype(BF16)
+
+        def grad_block(s):
             whole = lax.dot_general(
                 lows[rows_of(s), 0:columns],
                 vw[layer],
@@ -567,32 +687,64 @@
             )
             part[rows_of(s)] = whole.astype(BF16)
 
-        for step in far_first:
-            block(send.peer(step))
-            send.send(step)
-        block(x)
-
         def put(i, block):
             wt[layer, 0, i] = block[:, 0:columns].reshape(wt.shape[3:])
             wt[layer, 1, i] = block[:, columns:].reshape(wt.shape[3:])
 
-        weight_term(gath.at[layer], lows, put)
-        scatter = Scatter(layer)
-        scatter.start()
-        after_send(scatter, tap_total)
-        send.finish()
-        return scatter, tap_total
+        def weights():
+            weight_term(gath.at[layer], lows, put)
+            scatters[-1].start()
+
+        def block(s):
+            if not weights_first:
+                lows_block(s)
+            grad_block(s)
+
+        if weights_first:
+            lax.fori_loop(0, tp, lambda s, carry: lows_block(s) or carry, 0)
+            weights()
+        block(far)
+        send.send_far()
+        block(right)
+        block(left)
+        send.send_early()
+        block(x)
+        after_send(scatters, tap_total)
+        send.combine_first()
+        send.combine_last()
+        if not weights_first:
+            weights()
+        return send, scatters, tap_total
 
     tapsum[...] = jnp.zeros(tapsum.shape, F32)
-    normalize(0, lambda first_row, at: frames[at].astype(F32))
-    gather_up = gather_x(ups, 1)
+    fill(frames, hid)
+    gather = GatherX(gath, 0)
+    for group in (0, 1):
+        pair(group, lambda first_row: normalize(0, lambda r: rows_in(hid, r), first_row))
+    pl.semaphore_wait(barrier, len(peers))
+    for i in (0, 2, 1, 3):
+        gather.push(i)
+    fill(og, up)
+    gather_up = GatherX(ups, 1)
+
+    def copy_up(first_row):
+        ups[1, rows_of(x, first_row, CHUNK)] = rows_in(up, first_row).astype(BF16)
+
+    for group in (0, 1):
+        pair(group, copy_up)
+    for load in loads:
+        load.wait()
 
     def send_up():
-        ups[1, rows_of(x)] = og[...]
-        gather_up.start()
-
-    activate, scale0 = forward(0, send_up)
-    branch = scatter_x(0)
+        for i in (0, 2, 1, 3):
+            gather_up.push(i)
+
+    def up_onward():
+        for i in (0, 2, 1, 3):
+            gather_up.onward(i)
+
+    activate, scale0 = forward(0, gather, send_up, up_onward)
+    branch = ScatterX(0)
 
     def project_block(s):
         activate(s)
@@ -600,59 +752,104 @@
             act[0, rows_of(s)], pw[0], preferred_element_type=F32
         ).astype(BF16)
 
-    for step in far_first:
-        project_block(branch.peer(step))
-        branch.send(step)
+    project_block(far)
+    branch.send_far()
+    project_block(right)
+    project_block(left)
+    branch.send_early()
     project_block(x)
-    branch.finish()
-
-    def hidden(first_row, at):
-        return (frames[at].astype(F32) + landed_sum(0, first_row)).astype(BF16).astype(F32)
-
-    normalize(1, hidden)
-    activate, scale1 = forward(1)
-    gather_up.finish()
+    branch.combine_first()
+    branch.combine_last()
+
+    def hidden(first_row):
+        return (rows_in(hid, first_row) + branch.rows(first_row)).astype(BF16).astype(F32)
+
+    gather = GatherX(gath, 1)
+    for group in (0, 1):
+        branch.landed(group)
+        branch.landed(group + 2)
+        pair(group, lambda first_row: normalize(1, hidden, first_row))
+        gather.push(group)
+        gather.push(group + 2)
+    branch.sent()
+
+    def nothing():
+        return None
+
+    activate, scale1 = forward(1, gather, nothing, None)
+    gather_up.wait_left()
+    gather_up.wait_right()
+    gather_up.wait_far()
+    gather_up.sent()
 
     def all_blocks(block, carry):
         return lax.fori_loop(0, tp, block, carry)
 
-    scatter1, taps1 = backward(
-        1, 1, all_blocks, scale1, activate, lambda: None, lambda scatter, tap_total: tap_total.middle()
+    send, (scatter1,), taps1 = backward(
+        1, 1, all_blocks, scale1, activate, nothing, lambda scatters, tap_total: tap_total.middle(), False
     )
-
-    def next_up(i, at, grad):
-        whole = og[at].astype(F32) + grad
-        up[at] = whole
-        ups[0, rows_of(x, i * CHUNK, CHUNK)] = whole.astype(BF16)
-
-    back_rows(1, 1, next_up)
-    gather0 = gather_x(ups, 0)
-    gather0.start()
-    scatter1.after_core()
-    taps1.finish()
+    gather0 = GatherX(ups, 0)
+
+    def next_up(first_row):
+        whole = rows_in(up, first_row) + back_rows(1, send, first_row)
+        up[tiles(first_row)] = whole.reshape(CHUNK // 8, 8, depth)
+        ups[0, rows_of(x, first_row, CHUNK)] = whole.astype(BF16)
+
+    for group in (0, 1):
+        send.landed(group)
+        send.landed(group + 2)
+        pair(group, next_up)
+        gather0.push(group)
+        gather0.push(group + 2)
 
     def in_turn(block, carry):
+        gather0.onward(0)
+        gather0.onward(2)
         carry = block(x, carry)
-        for step in far_last:
-            gather0.landed(step)
-            carry = block(gather0.peer(step), carry)
+        gather0.onward(1)
+        gather0.onward(3)
+        scatter1.after_core()
+        send.sent()
+        taps1.finish()
+        gather0.wait_left()
+        carry = block(left, carry)
+        gather0.wait_right()
+        carry = block(right, carry)
+        gather0.wait_far()
+        carry = block(far, carry)
         gather0.sent()
         return carry
 
-    def finish_first(scatter, tap_total):
+    def finish_first(scatters, tap_total):
         tap_total.middle()
-        scatter.after_core()
+        scatters[0].after_z()
         scatter1.after_z()
-
-    scatter0, taps0 = backward(0, 2, in_turn, scale0, None, scatter1.after_y, finish_first)
-
-    def last_up(i, at, grad):
-        up[at] = up[at] + grad
-
-    back_rows(0, 2, last_up)
-    scatter0.after_y()
+        scatters[1].after_core()
+
+    last, scatters0, taps0 = backward(
+        0, 2, in_turn, scale0, None, scatter1.after_y, finish_first, True
+    )
+
+    def last_up(first_row):
+        whole = rows_in(up, first_row) + back_rows(0, last, first_row)
+        up[tiles(first_row)] = whole.reshape(CHUNK // 8, 8, depth)
+
+        def put(i, carry):
+            t = first_row // 8 + i
+            for q in range(STREAMS):
+                up_out[q, t] = up[t, 2 * q : 2 * q + 2, :]
+            return carry
+
+        lax.fori_loop(0, CHUNK // 8, put, 0)
+
+    for group in (0, 1):
+        last.landed(group)
+        last.landed(group + 2)
+        pair(group, last_up)
+    last.sent()
+    scatters0[1].after_y()
     taps0.finish()
-    scatter0.after_z()
+    scatters0[1].after_z()
 
 
 def scratch(ctx, tp, layers, depth, columns):
@@ -660,11 +857,17 @@
     rows = tp * ROWS
     piece = depth // ctx
     return [
+        pltpu.VMEM((layers, depth, columns), BF16),
+        pltpu.VMEM((layers, depth, columns), BF16),
+        pltpu.VMEM((layers, columns, depth), BF16),
+        pltpu.VMEM((SEG, 8, depth), F32),
+        pltpu.VMEM((SEG, 8, depth), F32),
         pltpu.VMEM((tp, ROWS, LANES), F32),
         pltpu.VMEM((layers, rows, depth), BF16),
         pltpu.VMEM((layers, rows, depth), BF16),
         pltpu.VMEM((rows, depth), BF16),
-        pltpu.VMEM((3, rows, depth), BF16),
+        pltpu.VMEM((3, ROWS, depth), BF16),
+        pltpu.VMEM((3, 2, ROWS, depth), BF16),
         pltpu.VMEM((layers, ROWS, depth), F32),
         pltpu.VMEM((layers, ROWS, LANES), F32),
         pltpu.VMEM((layers, 2, tp, ROWS, LANES), F32),
@@ -687,23 +890,10 @@
         pltpu.VMEM((layers, ny, 3, nz, piece, columns), BF16),
         pltpu.VMEM((layers, 3, nz, piece, columns), BF16),
         pltpu.VMEM((layers, nz, 3, piece, columns), BF16),
-        pltpu.SemaphoreType.DMA((192,)),
-        pltpu.SemaphoreType.DMA((192,)),
+        pltpu.SemaphoreType.DMA((3,)),
+        pltpu.SemaphoreType.DMA((256,)),
+        pltpu.SemaphoreType.DMA((256,)),
     ]
-
-
-def shuffled(rows):
-    frames, recs, depth = rows.shape
-    return (
-        rows.reshape(STREAMS, SEG, recs, depth).transpose(1, 0, 2, 3).reshape(frames * recs, depth)
-    )
-
-
-def restored(rows, recs):
-    count, depth = rows.shape
-    return (
-        rows.reshape(SEG, STREAMS, recs, depth).transpose(1, 0, 2, 3).reshape(count // recs, recs, depth)
-    )
 
 
 def on_device(
@@ -722,33 +912,42 @@
     piece = depth // ctx
     vmem = pl.BlockSpec(memory_space=pltpu.VMEM)
     smem = pl.BlockSpec(memory_space=pltpu.SMEM)
+    hbm = pl.BlockSpec(memory_space=pl.ANY)
+    recs = frames.shape[1]
+    split = (STREAMS, SEG, recs, depth)
     up, value, gate, project, tap = pl.pallas_call(
         functools.partial(fused, ctx, tp),
         out_shape=(
-            jax.ShapeDtypeStruct((ROWS, depth), F32),
+            jax.ShapeDtypeStruct(split, F32),
             jax.ShapeDtypeStruct((layers, piece, columns), F32),
             jax.ShapeDtypeStruct((layers, piece, columns), F32),
             jax.ShapeDtypeStruct((layers, piece, columns), F32),
-            jax.ShapeDtypeStruct((layers, TAPS, columns), F32),
+            jax.ShapeDtypeStruct((TAPS, layers, columns), F32),
         ),
-        in_specs=[vmem, vmem, smem, vmem, vmem, vmem, vmem, vmem, vmem],
+        in_specs=[vmem, vmem, smem, hbm, hbm, hbm, vmem, vmem, vmem],
         out_specs=(vmem,) * 5,
         scratch_shapes=scratch(ctx, tp, layers, depth, columns),
         compiler_params=pltpu.CompilerParams(
             collective_id=0, has_side_effects=True, vmem_limit_bytes=60 * 1024 * 1024
         ),
     )(
-        shuffled(frames),
-        shuffled(output_grad),
+        frames.reshape(split),
+        output_grad.reshape(split),
         lengths,
         value_weight,
         gate_weight,
         project_weight,
-        tap_weights,
+        jnp.swapaxes(tap_weights, 0, 1),
         norm_gain,
         norm_shift,
     )
-    return restored(up, frames.shape[1]), value, gate, jnp.swapaxes(project, 1, 2), tap
+    return (
+        up.reshape(frames.shape),
+        value,
+        gate,
+        jnp.swapaxes(project, 1, 2),
+        jnp.swapaxes(tap, 0, 1),
+    )
 
 
 def solution(mesh):

time: 173 us -> 152 us (0.88)
  Pallas kernels: 162 us -> 147 us
  local copies, waits for them, and re-layouts: 9.72 us -> 4.51 us
    pallas_call x1, Pallas kernels: 162 us -> 147 us  [on_device(): pl.pallas_call(functools.partial(fused, ctx, tp), out_shape=(jax.ShapeDty...]
    reshape x5 -> x0, local copies, waits for them, and re-layouts: 4.36 us -> none  [the longest x4 3.01 us: shuffled(): rows.reshape(STREAMS, SEG, recs, depth).transpose(1, 0, 2, 3)]
    unnamed x15 -> x13, local copies, waits for them, and re-layouts: 4.52 us -> 4.51 us
where the time goes in v3:
time: 152 us
  Pallas kernels  147 us (97%)
  local copies, waits for them, and re-layouts  4.51 us (3%)
    pallas_call x1, Pallas kernels, on_device(): pl.pallas_call(functools.partial(fused, ctx, tp), out_shape=(jax.ShapeDty...  147 us
    unnamed x13, local copies, waits for them, and re-layouts  4.51 us

profile of v3, /device:TPU:1, one launch (start us, length us, event | category | flops | bytes accessed | tf_op | source)
XLA Modules:
  0.0 151.7 jit_solution(15414339587274579920)
XLA Ops:
  0.6 146.6 %shard_map.128 = (f32[4,16,2,1024]{3,2,1,0:T(2,128)}, f32[2,16,256]{2,1,0:T(8,128)}, f32[2,16,256]{2,1,0:T(8,128)}, f32[2,16,256]{2,1,0:T(8,128)}, f32[31,2,256]{2,1,0:T(2,128)}) custom-call(bf16[4,16,2,1024]{3,2,1,0:T(2,128)(2,1)} %bitcast.7, bf16[4,16,2,1024]{3,2,1,0:T(2,128)(2,1)} %bitcast.8, s32[2]{0:T(128)} %lengths.1, bf16[2,1024,256]{2,1,0:T(8,128)(2,1)} %vw_in.1, ...), custom_call_target="tpu_custom_call" | custom-call | tf_op jit(solution)/shard_map/pallas_call | solution.py:918
  147.2 0.0 copy-start.3
  147.2 1.9 %copy.19 = f32[64,2,1024]{2,1,0:T(2,128)} copy(f32[64,2,1024]{2,1,0:T(2,128)} %bitcast.6) | data formatting | bytes 1048576
  149.1 0.0 copy-done.3
  149.1 0.0 copy-start.2
  149.1 0.0 copy-start.1
  149.1 0.6 copy.20
  149.7 0.2 copy-done.2
  149.9 0.0 copy-start
  149.9 0.6 copy.21
  150.5 0.0 copy-done.1
  150.5 0.6 copy.22
  151.1 0.0 copy-done
  151.1 0.6 copy.23
Async XLA Ops:
  147.2 1.9 %copy-start.3 = (f32[2,16,256]{2,1,0:T(8,128)S(1)}, f32[2,16,256]{2,1,0:T(8,128)}, u32[]{:S(2)}) copy-start(f32[2,16,256]{2,1,0:T(8,128)} %get-tuple-element.21) | copy-start | bytes 98308
  149.1 0.8 copy-start.2
  149.1 1.4 copy-start.1
  149.9 1.2 copy-start

commit v4 on v3

--- a/solution.py
+++ b/solution.py
@@ -70,6 +70,7 @@
     wide,
     lows,
     halo,
+    halo2,
     first,
     second,
     tapsum,
@@ -81,6 +82,9 @@
     in2,
     out3,
     in3,
+    in2z,
+    out3z,
+    in3z,
     lsem,
     ssem,
     rsem,
@@ -299,9 +303,9 @@
     t_in = lax.broadcasted_iota(jnp.int32, (SEG, 8, LANES), 0)
     sub = lax.broadcasted_iota(jnp.int32, (SEG, 8, LANES), 1)
     limit = jnp.where(sub % 2 == 0, len0, len1)
-    for s in range(tp):
+    for s in range(-1, tp + 1):
         frame = start_frame + s * (STREAMS * SEG) + (sub // 2) * SEG + t_in
-        val[s] = jnp.where(frame < limit, 1.0, 0.0).astype(F32).reshape(ROWS, LANES)
+        val[tp + 1 if s == tp else s if s >= 0 else tp] = jnp.where(frame < limit, 1.0, 0.0).astype(F32).reshape(ROWS, LANES)
     span = tp * STREAMS * SEG
     total = (len0 + len1).astype(F32)
     local_count = (
@@ -370,28 +374,22 @@
         return result
 
     class Halo:
-        def __init__(self, u):
+        def __init__(self, u, src, dst):
             self.u = u
             base = take(2)
-            self.up = remote(
-                glu.at[rows_of(tp - 1)], halo.at[u, 0], base, base, following
-            )
-            self.down = remote(glu.at[rows_of(0)], halo.at[u, 1], base + 1, base + 1, previous)
+            self.up = remote(src.at[rows_of(tp - 1)], dst.at[u, 0], base, base, following)
+            self.down = remote(src.at[rows_of(0)], dst.at[u, 1], base + 1, base + 1, previous)
 
         def start(self):
             self.up.start()
             self.down.start()
 
-        def finish(self, e):
+        def wait(self):
             self.up.wait()
             self.down.wait()
-            has_low = (pos > 0).astype(F32)
-            has_high = (pos < ctx - 1).astype(F32)
-            for h in range(2):
-                wide[e, h, 0, MAIN : MAIN + ROWS] = halo[self.u, 0, :, halves(h)].astype(F32) * has_low
-                wide[e, h, tp + 1, MAIN : MAIN + ROWS] = (
-                    halo[self.u, 1, :, halves(h)].astype(F32) * has_high
-                )
+
+    has_low = (pos > 0).astype(F32)
+    has_high = (pos < ctx - 1).astype(F32)
 
     class Scatter:
         def __init__(self, layer, low, high):
@@ -450,11 +448,59 @@
                     whole = whole + in3[layer, lax.rem(z + s, nz), a].astype(F32)
                 out[layer] = whole
 
+    class CrossScatter:
+        def __init__(self, mat):
+            self.mat = mat
+            other = lax.rem(c + 1, nc)
+            base = take(1)
+            self.core = remote(
+                wt.at[0, mat, :, :, other], in1.at[0, mat], base, base, to_c(other)
+            )
+            self.zs = Exchange(
+                nz, z, to_z, lambda p: out2.at[0, mat, :, p], lambda p: in2z.at[p]
+            )
+            self.ys = Exchange(ny, y, to_y, lambda p: out3z.at[p], lambda p: in3z.at[p])
+
+        def start(self):
+            self.core.start()
+
+        def after_core(self):
+            self.core.wait()
+
+            def add(b, carry):
+                out2[0, self.mat, b] = (
+                    wt[0, self.mat, b, :, c].astype(F32) + in1[0, self.mat, b].astype(F32)
+                ).astype(BF16)
+                return carry
+
+            lax.fori_loop(0, ny, add, 0)
+            self.zs.start()
+
+        def after_z(self):
+            self.zs.finish()
+
+            def add(b, carry):
+                whole = out2[0, self.mat, b, z].astype(F32)
+                for s in range(1, nz):
+                    whole = whole + in2z[lax.rem(z + s, nz), b].astype(F32)
+                out3z[b] = whole.astype(BF16)
+                return carry
+
+            lax.fori_loop(0, ny, add, 0)
+            self.ys.start()
+
+        def after_y(self):
+            self.ys.finish()
+            whole = out3z[y].astype(F32)
+            for s in range(1, ny):
+                whole = whole + in3z[lax.rem(y + s, ny)].astype(F32)
+            gate_out[0] = whole
+
     def weight_term(left, right, put):
         def step(i, carry):
             cols = pl.ds(pl.multiple_of(i * (depth // ny), depth // ny), depth // ny)
             whole = lax.dot_general(
-                left[:, cols], right[...], (((0,), (0,)), ((), ())), preferred_element_type=F32
+                left[:, cols], right, (((0,), (0,)), ((), ())), preferred_element_type=F32
             )
             put(i, whole.astype(BF16))
             return carry
@@ -552,7 +598,7 @@
         block(right)
         gather.wait_far()
         block(far)
-        edge = Halo(layer)
+        edge = Halo(layer, glu, halo)
         edge.start()
 
         def conv(s, carry):
@@ -566,7 +612,12 @@
 
         zero = jnp.zeros((8, LANES), F32)
         sums = lax.fori_loop(1, tp - 1, conv, (zero, zero))
-        edge.finish(layer)
+        edge.wait()
+        for h in range(2):
+            wide[layer, h, 0, MAIN : MAIN + ROWS] = halo[layer, 0, :, halves(h)].astype(F32) * has_low
+            wide[layer, h, tp + 1, MAIN : MAIN + ROWS] = (
+                halo[layer, 1, :, halves(h)].astype(F32) * has_high
+            )
         sums = lax.fori_loop(0, 2, lambda i, carry: conv(i * (tp - 1), carry), sums)
         sums = [jnp.sum(v, axis=0, keepdims=True) for v in sums]
         means = [v / jnp.maximum(local_count, 1.0) for v in sums]
@@ -597,7 +648,7 @@
 
         return activate, scale
 
-    def backward(layer, u, up_block, chan_scale, activate, between, after_send, weights_first):
+    def backward(layer, u, up_block, chan_scale, activate, meanwhile, between, weights_first):
         zero = jnp.zeros((8, LANES), F32)
 
         def one_block(s, carry):
@@ -609,58 +660,85 @@
             sums = list(carry)
             for h in range(2):
                 g = grad[:, halves(h)] * ds[layer, h, s]
+                unit = scaled[layer, h, s]
                 ds[layer, h, s] = g
+                lows[rows_of(s), halves(h)] = g.astype(BF16)
+                lows[rows_of(s), halves(2 + h)] = unit.astype(BF16)
                 sums[h] = sums[h] + fold(g)
-                sums[2 + h] = sums[2 + h] + fold(g * scaled[layer, h, s])
+                sums[2 + h] = sums[2 + h] + fold(g * unit)
             return tuple(sums)
 
         sums = up_block(one_block, (zero,) * 4)
+        edge = Halo(layer, lows, halo2)
+        edge.start()
         sums = [jnp.sum(v, axis=0, keepdims=True) for v in sums]
 
-        scatters = [Scatter(layer, 2, 3), Scatter(layer, 0, 2)] if weights_first else [Scatter(layer, 0, 3)]
+        if weights_first:
+            scatters = [Scatter(layer, 2, 3), Scatter(layer, 0, 1), CrossScatter(1)]
+        else:
+            scatters = [Scatter(layer, 0, 3)]
 
         def project():
             def put(i, block):
                 wt[layer, 2, i] = block.reshape(wt.shape[3:])
 
-            weight_term(ups.at[layer], act.at[layer], put)
+            weight_term(ups.at[layer], act[layer], put)
             if weights_first:
                 scatters[0].start()
 
         whole = reduce_tile(2 + layer, sums, merge_sum, project)
+        meanwhile()
         if weights_first:
             scatters[0].after_core()
+        edge.wait()
+        factor = [gain[layer : layer + 1, halves(h)] * chan_scale[h] for h in range(2)]
+        first_mean = [whole[h : h + 1] / total for h in range(2)]
+        cross_mean = [whole[2 + h : 3 + h] / total for h in range(2)]
+
+        def mixed_grad(h, grad, unit, keep):
+            return factor[h] * (grad - first_mean[h] - unit * cross_mean[h]) * keep
 
         def mix(s, carry):
             for h in range(2):
-                factor = gain[layer : layer + 1, halves(h)] * chan_scale[h]
-                a, b = whole[h : h + 1] / total, whole[2 + h : 3 + h] / total
-                grad = factor * (ds[layer, h, s] - a - scaled[layer, h, s] * b) * val[s]
-                wide[2, h, s + 1, MAIN : MAIN + ROWS] = grad
-                glu[rows_of(s), halves(h)] = grad.astype(BF16)
+                wide[2, h, s + 1, MAIN : MAIN + ROWS] = mixed_grad(
+                    h, ds[layer, h, s], scaled[layer, h, s], val[s]
+                )
             return carry
 
         lax.fori_loop(0, tp, mix, 0)
-        edge = Halo(2 + layer)
-        edge.start()
-
-        def tap(j, carry):
-            at = pl.ds(pl.multiple_of(j * 8, 8), ROWS)
+        for side, has in enumerate((has_low, has_high)):
             for h in range(2):
-                whole = None
-                for s in range(1, tp + 1):
-                    term = fold(wide[layer, h, s, at] * wide[2, h, s, MAIN : MAIN + ROWS])
-                    whole = term if whole is None else whole + term
-                tapsum[h, pl.ds(j, 1), :] = jnp.sum(whole, axis=0, keepdims=True)
-            return carry
-
-        lax.fori_loop(0, TAPS, tap, 0)
-        tap_total = TapSum(layer)
-        edge.finish(2)
-        tap_total.start()
-        between()
-        if weights_first:
-            scatters[0].after_y()
+                wide[2, h, side * (tp + 1), MAIN : MAIN + ROWS] = mixed_grad(
+                    h,
+                    halo2[layer, side, :, halves(h)].astype(F32),
+                    halo2[layer, side, :, halves(2 + h)].astype(F32),
+                    val[tp + side] * has,
+                )
+
+        def tap_terms():
+            block = 8
+            for h in range(2):
+
+                def tap(i, sums):
+                    s, t = i // (SEG // block), i % (SEG // block) * block
+                    sums = list(sums)
+                    grads = [
+                        wide[2, h, s + 1, pl.ds(pl.multiple_of(MAIN + (t + k) * 8, 8), 8)]
+                        for k in range(block)
+                    ]
+                    for k in range(block + TAPS - 1):
+                        row = wide[layer, h, s + 1, pl.ds(pl.multiple_of((t + k) * 8, 8), 8)]
+                        for m in range(block):
+                            if 0 <= k - m < TAPS:
+                                sums[k - m] = sums[k - m] + row * grads[m]
+                    return tuple(sums)
+
+                sums = lax.fori_loop(0, tp * SEG // block, tap, (zero,) * TAPS)
+                for j in range(TAPS):
+                    tapsum[h, j : j + 1, :] = jnp.sum(sums[j], axis=0, keepdims=True)
+            total_taps = TapSum(layer)
+            total_taps.start()
+            return total_taps
 
         send = ScatterX(u)
 
@@ -687,13 +765,25 @@
             )
             part[rows_of(s)] = whole.astype(BF16)
 
-        def put(i, block):
-            wt[layer, 0, i] = block[:, 0:columns].reshape(wt.shape[3:])
-            wt[layer, 1, i] = block[:, columns:].reshape(wt.shape[3:])
-
         def weights():
-            weight_term(gath.at[layer], lows, put)
-            scatters[-1].start()
+            if weights_first:
+                for m in range(2):
+
+                    def put_one(i, block):
+                        wt[layer, m, i] = block.reshape(wt.shape[3:])
+
+                    weight_term(gath.at[layer], lows[:, m * columns : (m + 1) * columns], put_one)
+                    scatters[1 + m].start()
+                    if m == 1:
+                        scatters[1].after_core()
+            else:
+
+                def put(i, block):
+                    wt[layer, 0, i] = block[:, 0:columns].reshape(wt.shape[3:])
+                    wt[layer, 1, i] = block[:, columns:].reshape(wt.shape[3:])
+
+                weight_term(gath.at[layer], lows[...], put)
+                scatters[0].start()
 
         def block(s):
             if not weights_first:
@@ -705,16 +795,18 @@
             weights()
         block(far)
         send.send_far()
+        if weights_first:
+            scatters[2].after_core()
         block(right)
         block(left)
         send.send_early()
+        between()
         block(x)
-        after_send(scatters, tap_total)
         send.combine_first()
         send.combine_last()
         if not weights_first:
             weights()
-        return send, scatters, tap_total
+        return send, scatters, tap_terms
 
     tapsum[...] = jnp.zeros(tapsum.shape, F32)
     fill(frames, hid)
@@ -785,8 +877,8 @@
     def all_blocks(block, carry):
         return lax.fori_loop(0, tp, block, carry)
 
-    send, (scatter1,), taps1 = backward(
-        1, 1, all_blocks, scale1, activate, nothing, lambda scatters, tap_total: tap_total.middle(), False
+    send, (scatter1,), tap_terms1 = backward(
+        1, 1, all_blocks, scale1, activate, nothing, nothing, False
     )
     gather0 = GatherX(ups, 0)
 
@@ -801,6 +893,9 @@
         pair(group, next_up)
         gather0.push(group)
         gather0.push(group + 2)
+        if group == 0:
+            scatter1.after_core()
+    taps1 = []
 
     def in_turn(block, carry):
         gather0.onward(0)
@@ -808,9 +903,8 @@
         carry = block(x, carry)
         gather0.onward(1)
         gather0.onward(3)
-        scatter1.after_core()
         send.sent()
-        taps1.finish()
+        taps1.append(tap_terms1())
         gather0.wait_left()
         carry = block(left, carry)
         gather0.wait_right()
@@ -820,15 +914,11 @@
         gather0.sent()
         return carry
 
-    def finish_first(scatters, tap_total):
-        tap_total.middle()
-        scatters[0].after_z()
-        scatter1.after_z()
-        scatters[1].after_core()
-
-    last, scatters0, taps0 = backward(
-        0, 2, in_turn, scale0, None, scatter1.after_y, finish_first, True
+    last, scatters0, tap_terms0 = backward(
+        0, 2, in_turn, scale0, None, lambda: taps1[0].middle(), scatter1.after_y, True
     )
+    taps0 = tap_terms0()
+    scatters0[0].after_y()
 
     def last_up(first_row):
         whole = rows_in(up, first_row) + back_rows(0, last, first_row)
@@ -842,14 +932,22 @@
 
         lax.fori_loop(0, CHUNK // 8, put, 0)
 
-    for group in (0, 1):
-        last.landed(group)
-        last.landed(group + 2)
-        pair(group, last_up)
+    scatters0[1].after_y()
+    last.landed(0)
+    last.landed(2)
+    pair(0, last_up)
+    taps0.middle()
+    scatters0[2].after_z()
+    last.landed(1)
+    last.landed(3)
+    pair(1, last_up)
     last.sent()
-    scatters0[1].after_y()
+    taps1[0].finish()
+    scatter1.after_z()
+    scatters0[0].after_z()
+    scatters0[1].after_z()
+    scatters0[2].after_y()
     taps0.finish()
-    scatters0[1].after_z()
 
 
 def scratch(ctx, tp, layers, depth, columns):
@@ -862,7 +960,7 @@
         pltpu.VMEM((layers, columns, depth), BF16),
         pltpu.VMEM((SEG, 8, depth), F32),
         pltpu.VMEM((SEG, 8, depth), F32),
-        pltpu.VMEM((tp, ROWS, LANES), F32),
+        pltpu.VMEM((tp + 2, ROWS, LANES), F32),
         pltpu.VMEM((layers, rows, depth), BF16),
         pltpu.VMEM((layers, rows, depth), BF16),
         pltpu.VMEM((rows, depth), BF16),
@@ -878,7 +976,8 @@
         pltpu.VMEM((rows, columns), BF16),
         pltpu.VMEM((3, 2, tp + 2, WIDE, LANES), F32),
         pltpu.VMEM((rows, 2 * columns), BF16),
-        pltpu.VMEM((4, 2, ROWS, columns), BF16),
+        pltpu.VMEM((layers, 2, ROWS, columns), BF16),
+        pltpu.VMEM((layers, 2, ROWS, 2 * columns), BF16),
         pltpu.VMEM((4, ny * nc, 8, LANES), F32),
         pltpu.VMEM((4, nz, 8, LANES), F32),
         pltpu.VMEM((2, TAPS + 1, LANES), F32),
@@ -890,10 +989,19 @@
         pltpu.VMEM((layers, ny, 3, nz, piece, columns), BF16),
         pltpu.VMEM((layers, 3, nz, piece, columns), BF16),
         pltpu.VMEM((layers, nz, 3, piece, columns), BF16),
+        pltpu.VMEM((nz, ny, piece, columns), BF16),
+        pltpu.VMEM((ny, piece, columns), BF16),
+        pltpu.VMEM((ny, piece, columns), BF16),
         pltpu.SemaphoreType.DMA((3,)),
         pltpu.SemaphoreType.DMA((256,)),
         pltpu.SemaphoreType.DMA((256,)),
     ]
+
+
+def flush(*refs):
+    count = len(refs) // 2
+    for i in range(count):
+        refs[count + i][...] = refs[i][...]
 
 
 def on_device(
@@ -915,15 +1023,16 @@
     hbm = pl.BlockSpec(memory_space=pl.ANY)
     recs = frames.shape[1]
     split = (STREAMS, SEG, recs, depth)
-    up, value, gate, project, tap = pl.pallas_call(
+    shapes = (
+        jax.ShapeDtypeStruct(split, F32),
+        jax.ShapeDtypeStruct((layers, piece, columns), F32),
+        jax.ShapeDtypeStruct((layers, piece, columns), F32),
+        jax.ShapeDtypeStruct((layers, piece, columns), F32),
+        jax.ShapeDtypeStruct((TAPS, layers, columns), F32),
+    )
+    results = pl.pallas_call(
         functools.partial(fused, ctx, tp),
-        out_shape=(
-            jax.ShapeDtypeStruct(split, F32),
-            jax.ShapeDtypeStruct((layers, piece, columns), F32),
-            jax.ShapeDtypeStruct((layers, piece, columns), F32),
-            jax.ShapeDtypeStruct((layers, piece, columns), F32),
-            jax.ShapeDtypeStruct((TAPS, layers, columns), F32),
-        ),
+        out_shape=shapes,
         in_specs=[vmem, vmem, smem, hbm, hbm, hbm, vmem, vmem, vmem],
         out_specs=(vmem,) * 5,
         scratch_shapes=scratch(ctx, tp, layers, depth, columns),
@@ -941,6 +1050,12 @@
         norm_gain,
         norm_shift,
     )
+    up, value, gate, project, tap = pl.pallas_call(
+        flush,
+        out_shape=shapes,
+        in_specs=[vmem] * 5,
+        out_specs=(vmem,) * 5,
+    )(*results)
     return (
         up.reshape(frames.shape),
         value,

time: 152 us -> 140 us (0.921)
  Pallas kernels: 147 us -> 139 us
  local copies, waits for them, and re-layouts: 4.51 us -> 0 us
    pallas_call x1 -> x2, Pallas kernels: 147 us -> 139 us  [the longest x1 137 us: on_device(): pl.pallas_call(functools.partial(fused, ctx, tp), out_shape=shapes, in_sp...]
    unnamed x13 -> x0, local copies, waits for them, and re-layouts: 4.51 us -> none
where the time goes in v4:
time: 140 us
  Pallas kernels  139 us (99%)
    pallas_call x1, Pallas kernels, on_device(): pl.pallas_call(functools.partial(fused, ctx, tp), out_shape=shapes, in_sp...  137 us

profile of v4, /device:TPU:1, one launch (start us, length us, event | category | flops | bytes accessed | tf_op | source)
XLA Modules:
  0.0 139.7 jit_solution(18407287349673701758)
XLA Ops:
  0.6 137.1 %shard_map.128 = (f32[4,16,2,1024]{3,2,1,0:T(2,128)}, f32[2,16,256]{2,1,0:T(8,128)}, f32[2,16,256]{2,1,0:T(8,128)}, f32[2,16,256]{2,1,0:T(8,128)}, f32[31,2,256]{2,1,0:T(2,128)}) custom-call(bf16[4,16,2,1024]{3,2,1,0:T(2,128)(2,1)} %bitcast.6, bf16[4,16,2,1024]{3,2,1,0:T(2,128)(2,1)} %bitcast.7, s32[2]{0:T(128)} %lengths.1, bf16[2,1024,256]{2,1,0:T(8,128)(2,1)} %vw_in.1, ...), custom_call_target="tpu_custom_call" | custom-call | tf_op jit(solution)/shard_map/pallas_call | solution.py:1033
  137.8 1.9 %shard_map.129 = (f32[4,16,2,1024]{3,2,1,0:T(2,128)}, f32[2,16,256]{2,1,0:T(8,128)}, f32[2,16,256]{2,1,0:T(8,128)}, f32[2,16,256]{2,1,0:T(8,128)}, f32[31,2,256]{2,1,0:T(2,128)}) custom-call(f32[4,16,2,1024]{3,2,1,0:T(2,128)} %get-tuple-element.15.refs_0_, f32[2,16,256]{2,1,0:T(8,128)} %get-tuple-element.16.refs_1_, ...), custom_call_target="tpu_custom_call" | custom-call | tf_op jit(solution)/shard_map/pallas_call | solution.py:1053

commit v5 on v4

--- a/solution.py
+++ b/solution.py
@@ -34,16 +34,16 @@
 def fused(
     ctx,
     tp,
-    frames,
-    og,
+    frames_in,
+    og_in,
     lengths,
     vw_in,
     gw_in,
     pw_in,
-    taps,
-    gain,
-    shift,
-    up_out,
+    taps_in,
+    gain_in,
+    shift_in,
+    up,
     value_out,
     gate_out,
     project_out,
@@ -51,8 +51,12 @@
     vw,
     gw,
     pw,
+    frames,
+    og,
+    taps,
+    gain,
+    shift,
     hid,
-    up,
     val,
     gath,
     ups,
@@ -82,6 +86,7 @@
     in2,
     out3,
     in3,
+    early,
     in2z,
     out3z,
     in3z,
@@ -115,6 +120,24 @@
     following = {"ctx": lax.rem(pos + 1, ctx)}
     previous = {"ctx": lax.rem(pos + ctx - 1, ctx)}
 
+    loads = [
+        pltpu.make_async_copy(src, dst, lsem.at[i])
+        for i, (src, dst) in enumerate(
+            (
+                (frames_in, frames),
+                (og_in, og),
+                (vw_in, vw),
+                (gw_in, gw),
+                (taps_in, taps),
+                (gain_in, gain),
+                (shift_in, shift),
+                (pw_in, pw),
+            )
+        )
+    ]
+    for load in loads:
+        load.start()
+
     barrier = pltpu.get_barrier_semaphore()
     peers = [to_x(lax.rem(x + s, tp)) for s in range(1, tp)]
     peers += [to_yc(lax.rem(yc + s, ny * nc)) for s in range(1, ny * nc)]
@@ -122,13 +145,6 @@
     peers += [following, previous]
     for peer in peers:
         pl.semaphore_signal(barrier, inc=1, device_id=peer, device_id_type=MESH)
-    loads = [
-        pltpu.make_async_copy(src, dst, lsem.at[i])
-        for i, (src, dst) in enumerate(((vw_in, vw), (gw_in, gw), (pw_in, pw)))
-    ]
-    for load in loads:
-        load.start()
-
     taken = [0]
 
     def take(n):
@@ -611,14 +627,39 @@
             return tuple(sums)
 
         zero = jnp.zeros((8, LANES), F32)
-        sums = lax.fori_loop(1, tp - 1, conv, (zero, zero))
+        for h in range(2):
+            for side in (0, tp + 1):
+                wide[layer, h, side, MAIN : MAIN + ROWS] = jnp.zeros((ROWS, LANES), F32)
+        sums = list(lax.fori_loop(0, tp, conv, (zero, zero)))
         edge.wait()
         for h in range(2):
-            wide[layer, h, 0, MAIN : MAIN + ROWS] = halo[layer, 0, :, halves(h)].astype(F32) * has_low
-            wide[layer, h, tp + 1, MAIN : MAIN + ROWS] = (
-                halo[layer, 1, :, halves(h)].astype(F32) * has_high
-            )
-        sums = lax.fori_loop(0, 2, lambda i, carry: conv(i * (tp - 1), carry), sums)
+            tap_rows = [taps[j, layer : layer + 1, halves(h)] for j in range(TAPS)]
+            low = halo[layer, 0, :, halves(h)].astype(F32) * has_low
+            high = halo[layer, 1, :, halves(h)].astype(F32) * has_high
+            wide[layer, h, 0, MAIN : MAIN + ROWS] = low
+            wide[layer, h, tp + 1, MAIN : MAIN + ROWS] = high
+            low = low[8:].reshape(REACH, 8, LANES)
+            high = high[: MAIN].reshape(REACH, 8, LANES)
+            low = jnp.where(tile_sub < 2, pltpu.roll(low, 2, 1), 0.0)
+            high = jnp.where(tile_sub >= 6, pltpu.roll(high, 6, 1), 0.0)
+            wide[layer, h, 1, 0:MAIN] += low.reshape(MAIN, LANES)
+            wide[layer, h, tp, MAIN + ROWS : WIDE] += high.reshape(MAIN, LANES)
+            for t in range(REACH):
+                at = slice(t * 8, t * 8 + 8)
+                add = None
+                for j in range(REACH - t):
+                    term = tap_rows[j] * low[t + j]
+                    add = term if add is None else add + term
+                scaled[layer, h, 0, at] += add
+                sums[h] = sums[h] + add * val[0, at]
+            for t in range(1, SEG):
+                at = slice(t * 8, t * 8 + 8)
+                add = None
+                for i in range(t):
+                    term = tap_rows[SEG + REACH + i - t] * high[i]
+                    add = term if add is None else add + term
+                scaled[layer, h, tp - 1, at] += add
+                sums[h] = sums[h] + add * val[tp - 1, at]
         sums = [jnp.sum(v, axis=0, keepdims=True) for v in sums]
         means = [v / jnp.maximum(local_count, 1.0) for v in sums]
 
@@ -648,15 +689,18 @@
 
         return activate, scale
 
+    def act_grad(layer, s):
+        return lax.dot_general(
+            ups[layer, rows_of(s)], pw[layer], (((1,), (1,)), ((), ())), preferred_element_type=F32
+        )
+
     def backward(layer, u, up_block, chan_scale, activate, meanwhile, between, weights_first):
         zero = jnp.zeros((8, LANES), F32)
 
         def one_block(s, carry):
             if activate is not None:
                 activate(s)
-            grad = lax.dot_general(
-                ups[layer, rows_of(s)], pw[layer], (((1,), (1,)), ((), ())), preferred_element_type=F32
-            )
+            grad = act_grad(layer, s) if activate is None else early[rows_of(s)]
             sums = list(carry)
             for h in range(2):
                 g = grad[:, halves(h)] * ds[layer, h, s]
@@ -687,9 +731,6 @@
                 scatters[0].start()
 
         whole = reduce_tile(2 + layer, sums, merge_sum, project)
-        meanwhile()
-        if weights_first:
-            scatters[0].after_core()
         edge.wait()
         factor = [gain[layer : layer + 1, halves(h)] * chan_scale[h] for h in range(2)]
         first_mean = [whole[h : h + 1] / total for h in range(2)]
@@ -792,14 +833,17 @@
 
         if weights_first:
             lax.fori_loop(0, tp, lambda s, carry: lows_block(s) or carry, 0)
-            weights()
         block(far)
         send.send_far()
         if weights_first:
-            scatters[2].after_core()
+            meanwhile()
+            scatters[0].after_core()
+            weights()
         block(right)
         block(left)
         send.send_early()
+        if weights_first:
+            scatters[2].after_core()
         between()
         block(x)
         send.combine_first()
@@ -809,6 +853,7 @@
         return send, scatters, tap_terms
 
     tapsum[...] = jnp.zeros(tapsum.shape, F32)
+    loads[0].wait()
     fill(frames, hid)
     gather = GatherX(gath, 0)
     for group in (0, 1):
@@ -816,6 +861,7 @@
     pl.semaphore_wait(barrier, len(peers))
     for i in (0, 2, 1, 3):
         gather.push(i)
+    loads[1].wait()
     fill(og, up)
     gather_up = GatherX(ups, 1)
 
@@ -824,7 +870,7 @@
 
     for group in (0, 1):
         pair(group, copy_up)
-    for load in loads:
+    for load in loads[2:]:
         load.wait()
 
     def send_up():
@@ -868,11 +914,19 @@
     def nothing():
         return None
 
-    activate, scale1 = forward(1, gather, nothing, None)
-    gather_up.wait_left()
-    gather_up.wait_right()
-    gather_up.wait_far()
-    gather_up.sent()
+    def early_products():
+        gather_up.wait_left()
+        gather_up.wait_right()
+        gather_up.wait_far()
+        gather_up.sent()
+
+        def step(s, carry):
+            early[rows_of(s)] = act_grad(1, s)
+            return carry
+
+        lax.fori_loop(0, tp, step, 0)
+
+    activate, scale1 = forward(1, gather, nothing, early_products)
 
     def all_blocks(block, carry):
         return lax.fori_loop(0, tp, block, carry)
@@ -924,14 +978,6 @@
         whole = rows_in(up, first_row) + back_rows(0, last, first_row)
         up[tiles(first_row)] = whole.reshape(CHUNK // 8, 8, depth)
 
-        def put(i, carry):
-            t = first_row // 8 + i
-            for q in range(STREAMS):
-                up_out[q, t] = up[t, 2 * q : 2 * q + 2, :]
-            return carry
-
-        lax.fori_loop(0, CHUNK // 8, put, 0)
-
     scatters0[1].after_y()
     last.landed(0)
     last.landed(2)
@@ -958,7 +1004,11 @@
         pltpu.VMEM((layers, depth, columns), BF16),
         pltpu.VMEM((layers, depth, columns), BF16),
         pltpu.VMEM((layers, columns, depth), BF16),
-        pltpu.VMEM((SEG, 8, depth), F32),
+        pltpu.VMEM((STREAMS, SEG, 2, depth), BF16),
+        pltpu.VMEM((STREAMS, SEG, 2, depth), BF16),
+        pltpu.VMEM((TAPS, layers, columns), F32),
+        pltpu.VMEM((layers, columns), F32),
+        pltpu.VMEM((layers, columns), F32),
         pltpu.VMEM((SEG, 8, depth), F32),
         pltpu.VMEM((tp + 2, ROWS, LANES), F32),
         pltpu.VMEM((layers, rows, depth), BF16),
@@ -989,10 +1039,11 @@
         pltpu.VMEM((layers, ny, 3, nz, piece, columns), BF16),
         pltpu.VMEM((layers, 3, nz, piece, columns), BF16),
         pltpu.VMEM((layers, nz, 3, piece, columns), BF16),
+        pltpu.VMEM((rows, columns), F32),
         pltpu.VMEM((nz, ny, piece, columns), BF16),
         pltpu.VMEM((ny, piece, columns), BF16),
         pltpu.VMEM((ny, piece, columns), BF16),
-        pltpu.SemaphoreType.DMA((3,)),
+        pltpu.SemaphoreType.DMA((8,)),
         pltpu.SemaphoreType.DMA((256,)),
         pltpu.SemaphoreType.DMA((256,)),
     ]
@@ -1000,8 +1051,15 @@
 
 def flush(*refs):
     count = len(refs) // 2
-    for i in range(count):
+    for i in range(1, count):
         refs[count + i][...] = refs[i][...]
+
+    def put(t, carry):
+        for q in range(STREAMS):
+            refs[count][q, t] = refs[0][t, 2 * q : 2 * q + 2, :]
+        return carry
+
+    lax.fori_loop(0, SEG, put, 0)
 
 
 def on_device(
@@ -1024,7 +1082,6 @@
     recs = frames.shape[1]
     split = (STREAMS, SEG, recs, depth)
     shapes = (
-        jax.ShapeDtypeStruct(split, F32),
         jax.ShapeDtypeStruct((layers, piece, columns), F32),
         jax.ShapeDtypeStruct((layers, piece, columns), F32),
         jax.ShapeDtypeStruct((layers, piece, columns), F32),
@@ -1032,8 +1089,8 @@
     )
     results = pl.pallas_call(
         functools.partial(fused, ctx, tp),
-        out_shape=shapes,
-        in_specs=[vmem, vmem, smem, hbm, hbm, hbm, vmem, vmem, vmem],
+        out_shape=(jax.ShapeDtypeStruct((SEG, 8, depth), F32),) + shapes,
+        in_specs=[hbm, hbm, smem] + [hbm] * 6,
         out_specs=(vmem,) * 5,
         scratch_shapes=scratch(ctx, tp, layers, depth, columns),
         compiler_params=pltpu.CompilerParams(
@@ -1052,7 +1109,7 @@
     )
     up, value, gate, project, tap = pl.pallas_call(
         flush,
-        out_shape=shapes,
+        out_shape=(jax.ShapeDtypeStruct(split, F32),) + shapes,
         in_specs=[vmem] * 5,
         out_specs=(vmem,) * 5,
     )(*results)

time: 140 us -> 138 us (0.986)
  Pallas kernels: 139 us -> 137 us
    pallas_call x2, Pallas kernels: 139 us -> 137 us  [the longest x1 135 us: on_device(): pl.pallas_call(functools.partial(fused, ctx, tp), out_shape=(jax.ShapeDty...]
where the time goes in v5:
time: 138 us
  Pallas kernels  137 us (99%)
    pallas_call x1, Pallas kernels, on_device(): pl.pallas_call(functools.partial(fused, ctx, tp), out_shape=(jax.ShapeDty...  135 us

profile of v5, /device:TPU:1, one launch (start us, length us, event | category | flops | bytes accessed | tf_op | source)
XLA Modules:
  0.0 137.6 jit_solution(8599768206816027045)
XLA Ops:
  0.6 134.9 %shard_map.128 = (f32[16,8,1024]{2,1,0:T(8,128)}, f32[2,16,256]{2,1,0:T(8,128)}, f32[2,16,256]{2,1,0:T(8,128)}, f32[2,16,256]{2,1,0:T(8,128)}, f32[31,2,256]{2,1,0:T(2,128)}) custom-call(bf16[4,16,2,1024]{3,2,1,0:T(2,128)(2,1)} %bitcast.6, bf16[4,16,2,1024]{3,2,1,0:T(2,128)(2,1)} %bitcast.7, s32[2]{0:T(128)} %lengths.1, bf16[2,1024,256]{2,1,0:T(8,128)(2,1)} %vw_in.1, ...), custom_call_target="tpu_custom_call" | custom-call | tf_op jit(solution)/shard_map/pallas_call | solution.py:1090
  135.5 2.1 %shard_map.129 = (f32[4,16,2,1024]{3,2,1,0:T(2,128)}, f32[2,16,256]{2,1,0:T(8,128)}, f32[2,16,256]{2,1,0:T(8,128)}, f32[2,16,256]{2,1,0:T(8,128)}, f32[31,2,256]{2,1,0:T(2,128)}) custom-call(f32[16,8,1024]{2,1,0:T(8,128)} %get-tuple-element.15.refs_0_, f32[2,16,256]{2,1,0:T(8,128)} %get-tuple-element.16.refs_1_, f32[2,16,256]{2,1,0:T(8,128)} %get-tuple-element.17.refs_2_, ...), custom_call_target="tpu_custom_call" | custom-call | tf_op jit(solution)/shard_map/pallas_call | solution.py:1110

commit v6 on v5

--- a/solution.py
+++ b/solution.py
@@ -607,7 +607,6 @@
         block(x)
         gather.onward(1)
         gather.onward(3)
-        after()
         gather.wait_left()
         block(left)
         gather.wait_right()
@@ -616,6 +615,7 @@
         block(far)
         edge = Halo(layer, glu, halo)
         edge.start()
+        after()
 
         def conv(s, carry):
             widen(layer, s + 1)

time: 138 us -> 138 us (level)
  no operation moved by 1% of the time
where the time goes in v6:
time: 138 us; the launch traced here: 137 us
  Pallas kernels  137 us (99%)
    pallas_call x1, Pallas kernels, on_device(): pl.pallas_call(functools.partial(fused, ctx, tp), out_shape=(jax.ShapeDty...  135 us

profile of v6, /device:TPU:1, one launch (start us, length us, event | category | flops | bytes accessed | tf_op | source)
XLA Modules:
  0.0 137.3 jit_solution(4164175991786613911)
XLA Ops:
  0.6 134.5 %shard_map.128 = (f32[16,8,1024]{2,1,0:T(8,128)}, f32[2,16,256]{2,1,0:T(8,128)}, f32[2,16,256]{2,1,0:T(8,128)}, f32[2,16,256]{2,1,0:T(8,128)}, f32[31,2,256]{2,1,0:T(2,128)}) custom-call(bf16[4,16,2,1024]{3,2,1,0:T(2,128)(2,1)} %bitcast.6, bf16[4,16,2,1024]{3,2,1,0:T(2,128)(2,1)} %bitcast.7, s32[2]{0:T(128)} %lengths.1, bf16[2,1024,256]{2,1,0:T(8,128)(2,1)} %vw_in.1, ...), custom_call_target="tpu_custom_call" | custom-call | tf_op jit(solution)/shard_map/pallas_call | solution.py:1090
  135.2 2.1 %shard_map.129 = (f32[4,16,2,1024]{3,2,1,0:T(2,128)}, f32[2,16,256]{2,1,0:T(8,128)}, f32[2,16,256]{2,1,0:T(8,128)}, f32[2,16,256]{2,1,0:T(8,128)}, f32[31,2,256]{2,1,0:T(2,128)}) custom-call(f32[16,8,1024]{2,1,0:T(8,128)} %get-tuple-element.15.refs_0_, f32[2,16,256]{2,1,0:T(8,128)} %get-tuple-element.16.refs_1_, f32[2,16,256]{2,1,0:T(8,128)} %get-tuple-element.17.refs_2_, ...), custom_call_target="tpu_custom_call" | custom-call | tf_op jit(solution)/shard_map/pallas_call | solution.py:1110
